TPU v7x, 32 devices: a whole 2x2x4 slice. The times are simulated.
32 devices in a mesh: runs: 2 (over x), space: 16 (over z, y, core).
Axes of the slice: x: 2, y: 2, z: 4, core: 2. Of those that a mesh axis runs over, the one named last changes fastest.
Arguments:
- phase_noise: float32 [32, 8, 16, 8, 128], P(('runs', 'space')), parts along dimension 0, may hold values from -0.9 to 0.9
- labels: int32 [64, 8, 128], P(('runs', 'space')), parts along dimension 0, may hold values from 0 to 63
- solute: float32 [64, 8, 128], P(('runs', 'space')), parts along dimension 0, may hold values from 0.05 to 0.95
- mobility: float32 [64], replicated, may hold values from 0.5 to 2
- phase_cotangent_blocks: float32 [32, 8, 16, 8, 128], P(('runs', 'space')), parts along dimension 0, may hold values from -6 to 6
- adj_solute: float32 [64, 8, 128], P(('runs', 'space')), parts along dimension 0, may hold values from -6 to 6
Outputs:
- grad_phase: float32 [32, 8, 16, 8, 128], P(('runs', 'space')), parts along dimension 0
- solute_gradient: float32 [64, 8, 128], P(('runs', 'space')), parts along dimension 0
- mobility_gradient: float32 [128], P('runs'), parts along dimension 0
There are 2 independent parts, one for each index of `runs`. A program takes and returns all parts, laid end to end along the dimension named above; an argument that names none is the same for every part. Nothing has to cross between parts.
All inputs are finite; a program needn't handle non-finite values.
Results may differ from a plain program's by a relative error of at most 0.000022.
Values sent between devices are 32-bit elements; how exact they have to be, the bound alone decides.
A program may use at most 64 MiB of HBM per device.

v0:
```python
import jax
import jax.numpy as jnp
from jax import lax
from jax.sharding import PartitionSpec as P

P_SIZE = 64
GROUPS = 8


time_step = 0.1
gradient_coef = 0.75
well_height = 1.0
coupling = 1.5
chem_height = 2.5
alpha_level = 0.2
beta_level = 0.8
solute_mobility = 0.3
epsilon = 1e-05


def swapped(block, axis, bit):
    count = lax.axis_size(axis)
    route = []
    for low in range(count):
        high = low | 1 << bit
        if high != low and high < count:
            route += [(low, high), (high, low)]
    return lax.ppermute(block, axis, route)


def from_behind(block, axis, distance):
    devices = range(lax.axis_size(axis))
    route = [((i - distance) % len(devices), i) for i in devices]
    return lax.ppermute(block, axis, route)


def upper_flag(position, level):
    return position // (1 << level) % 2 == 1


def react(phases, beta_mask, total, bsum, solute):
    denom = total + epsilon
    share = bsum / denom
    squares = phases * phases
    chem_slope = chem_height * ((solute - beta_level) ** 2 - (solute - alpha_level) ** 2)
    reaction = well_height * (phases**3 - phases + 2.0 * coupling * phases * (total - squares))
    return reaction + chem_slope * 2.0 * phases * (beta_mask - share) / denom


def potential_of(total, bsum, solute):
    share = bsum / (total + epsilon)
    return 2.0 * chem_height * (solute - alpha_level - share * (beta_level - alpha_level))


def order_total(fields):
    levels = GROUPS.bit_length() - 1
    for level in range(levels):
        fields = fields + swapped(fields, "space", level)
    return fields


def state_sums(phases, beta_mask):
    squares = phases * phases
    local = jnp.stack([jnp.sum(squares, axis=0), jnp.sum(squares * beta_mask, axis=0)])
    summed = order_total(local)
    return (summed[0], summed[1])


def z_rims(stacked):
    below = from_behind(stacked[:, -1:], "space", GROUPS)
    above = from_behind(stacked[:, :1], "space", -GROUPS)
    return jnp.concatenate([below, stacked, above], 1)


def laplace_rows(extended):
    middle = extended[:, 1:-1]
    result = extended[:, 2:] + extended[:, :-2] - 6.0 * middle
    result = result + jnp.roll(middle, 1, 2) + jnp.roll(middle, -1, 2)
    return result + jnp.roll(middle, 1, 3) + jnp.roll(middle, -1, 3)


def pull_state(state, beta_mask, reaction_bar, potential_bar):
    phases, total, bsum, solute = state

    def local_react(phase_in, total_in, bsum_in, solute_in):
        return react(phase_in, beta_mask, total_in, bsum_in, solute_in)

    unused, react_pull = jax.vjp(local_react, phases, total, bsum, solute)
    phase_bar, total_bar, bsum_bar, solute_bar = react_pull(reaction_bar)
    summed = order_total(jnp.stack([total_bar, bsum_bar, solute_bar]))
    unused_two, pot_pull = jax.vjp(potential_of, total, bsum, solute)
    total_pot, bsum_pot, solute_pot = pot_pull(potential_bar)
    total_all = summed[0] + total_pot
    bsum_all = summed[1] + bsum_pot
    phase_bar = phase_bar + 2.0 * phases * (total_all + beta_mask * bsum_all)
    return (phase_bar, summed[2] + solute_pot)


def backward_step(adj_fields, adj_conc, step_rate, state, beta_mask):
    weighted = step_rate * adj_fields
    stacked = jnp.concatenate([weighted, adj_conc[None]], 0)
    curvature = laplace_rows(z_rims(stacked))
    potential_bar = time_step * solute_mobility * curvature[-1]
    field_bar, conc_bar = pull_state(state, beta_mask, -weighted, potential_bar)
    return (adj_fields + field_bar + gradient_coef * curvature[:-1], adj_conc + conc_bar)


def body(phase_noise, labels, solute, mobility, phase_cotangent_blocks, adj_solute):
    position = lax.axis_index("space")
    group = position % GROUPS
    levels = GROUPS.bit_length() - 1
    local_orders = phase_noise.shape[1]
    sub_rows = labels.shape[0]
    label_slab = labels
    for level in range(levels):
        other = swapped(label_slab, "space", level)
        upper = upper_flag(position, level)
        label_slab = jnp.where(
            upper, jnp.concatenate([other, label_slab], 0), jnp.concatenate([label_slab, other], 0)
        )
    pair_slab = jnp.stack([solute, adj_solute])
    for level in range(levels):
        other = swapped(pair_slab, "space", level)
        upper = upper_flag(position, level)
        pair_slab = jnp.where(
            upper, jnp.concatenate([other, pair_slab], 1), jnp.concatenate([pair_slab, other], 1)
        )
    conc = pair_slab[0]
    adj_conc = pair_slab[1]
    order_ids = group * local_orders + lax.broadcasted_iota(jnp.int32, (local_orders, 1, 1, 1), 0)
    beta_mask = (order_ids >= P_SIZE // 2).astype(jnp.float32)
    phases = phase_noise[0] + 0.5 * (label_slab[None] == order_ids).astype(jnp.float32)
    local_mobility = lax.dynamic_slice_in_dim(mobility, group * local_orders, local_orders, 0)
    step_rate = (time_step * local_mobility)[:, None, None, None]
    total_start, bsum_start = state_sums(phases, beta_mask)
    reaction_start = react(phases, beta_mask, total_start, bsum_start, conc)
    potential_start = potential_of(total_start, bsum_start, conc)
    drive_start = reaction_start - gradient_coef * laplace_rows(z_rims(phases))
    phases_next = phases - step_rate * drive_start
    curves = laplace_rows(z_rims(jnp.concatenate([phases_next, potential_start[None]], 0)))
    curve_next = curves[:-1]
    conc_next = conc + time_step * solute_mobility * curves[-1]
    total_next, bsum_next = state_sums(phases_next, beta_mask)
    reaction_next = react(phases_next, beta_mask, total_next, bsum_next, conc_next)
    drive_next = reaction_next - gradient_coef * curve_next
    adj_local = phase_cotangent_blocks[0]
    phase_bar, conc_bar = backward_step(
        adj_local, adj_conc, step_rate, (phases_next, total_next, bsum_next, conc_next), beta_mask
    )
    grad_fields, grad_conc = backward_step(
        phase_bar, conc_bar, step_rate, (phases, total_start, bsum_start, conc), beta_mask
    )
    partial_terms = -time_step * (
        jnp.sum(adj_local * drive_next, axis=(1, 2, 3))
        + jnp.sum(phase_bar * drive_start, axis=(1, 2, 3))
    )
    placed = lax.dynamic_update_slice_in_dim(
        jnp.zeros((mobility.shape[0],), jnp.float32), partial_terms, group * local_orders, 0
    )
    mobility_gradient = lax.psum(placed, "space")
    solute_gradient = lax.dynamic_slice_in_dim(grad_conc, group * sub_rows, sub_rows, 0)
    return (grad_fields[None], solute_gradient, mobility_gradient)


def solution(mesh):
    return jax.shard_map(
        body,
        mesh=mesh,
        in_specs=(
            P(("runs", "space"), None, None, None, None),
            P(("runs", "space"), None, None),
            P(("runs", "space"), None, None),
            P(),
            P(("runs", "space"), None, None, None, None),
            P(("runs", "space"), None, None),
        ),
        out_specs=(
            P(("runs", "space"), None, None, None, None),
            P(("runs", "space"), None, None),
            P("runs"),
        ),
        check_vma=False,
    )
```

profile of v0, /device:TPU:0, one launch (start us, length us, event | category | flops | bytes accessed | tf_op | source)
XLA Modules:
  0.0 114.6 jit_solution(5604454374450935729)
XLA Ops:
  3.5 2.9 %collective-permute-start.4 = (s32[4,8,128]{2,1,0:T(8,128)S(1)}, s32[4,8,128]{2,1,0:T(8,128)S(1)}, u32[]{:S(2)}, u32[]{:S(2)}) collective-permute-start(s32[4,8,128]{2,1,0:T(8,128)S(1)} %add_select_fusion.2), channel_id=1, source_target_pairs={{0,2},{2,0},{1,3},{3,1},{4,6},{6,4},{5,7},{7,5},{8,10},{10,8},{9,1... | collective-permute-start | bytes 49160 | tf_op jit(solution)/shard_map/ppermute | solution.py:28
  7.2 0.9 collective-permute-done.4
  8.1 2.1 %collective-permute-start.5 = (s32[8,8,128]{2,1,0:T(8,128)S(1)}, s32[8,8,128]{2,1,0:T(8,128)S(1)}, u32[]{:S(2)}, u32[]{:S(2)}) collective-permute-start(s32[8,8,128]{2,1,0:T(8,128)S(1)} %add_select_fusion.1), channel_id=1, source_target_pairs={{0,4},{4,0},{1,5},{5,1},{2,6},{6,2},{3,7},{7,3},{8,12},{12,8},{9,1... | collective-permute-start | bytes 98312 | tf_op jit(solution)/shard_map/ppermute | solution.py:28
  10.2 0.9 collective-permute-done.1
  11.1 1.6 %collective-permute-start.2 = (f32[2,8,8,128]{3,2,1,0:T(8,128)S(1)}, f32[2,8,8,128]{3,2,1,0:T(8,128)S(1)}, u32[]{:S(2)}, u32[]{:S(2)}) collective-permute-start(f32[2,8,8,128]{3,2,1,0:T(8,128)S(1)} %maximum_select_fusion.1), channel_id=1, source_target_pairs={{0,4},{4,0},{1,5},{5,1},{2,6},{6,2},{3,7},{7,3},{8,12},{12,8},{9,1... | collective-permute-start | bytes 196616 | tf_op jit(solution)/shard_map/ppermute | solution.py:28
  13.6 1.1 collective-permute-done.6
  14.7 1.5 %collective-permute-start.7 = (f32[2,16,8,128]{3,2,1,0:T(8,128)S(1)}, f32[2,16,8,128]{3,2,1,0:T(8,128)S(1)}, u32[]{:S(2)}, u32[]{:S(2)}) collective-permute-start(f32[2,16,8,128]{3,2,1,0:T(8,128)S(1)} %fusion.102), channel_id=1, source_target_pairs={{0,2},{2,0},{1,3},{3,1},{4,6},{6,4},{5,7},{7,5},{8,10},{10,8},{9,1... | collective-permute-start | bytes 393224 | tf_op jit(solution)/shard_map/ppermute | solution.py:28
  16.4 4.0 %collective-permute-done.7 = f32[2,16,8,128]{3,2,1,0:T(8,128)S(1)} collective-permute-done((f32[2,16,8,128]{3,2,1,0:T(8,128)S(1)}, f32[2,16,8,128]{3,2,1,0:T(8,128)S(1)}, u32[]{:S(2)}, u32[]{:S(2)}) %collective-permute-start.7) | collective-permute-done | bytes 131104 | tf_op jit(solution)/shard_map/ppermute | solution.py:28
  20.4 1.6 %collective-permute-start.8 = (f32[2,16,8,128]{3,2,1,0:T(8,128)S(1)}, f32[2,16,8,128]{3,2,1,0:T(8,128)S(1)}, u32[]{:S(2)}, u32[]{:S(2)}) collective-permute-start(f32[2,16,8,128]{3,2,1,0:T(8,128)S(1)} %fusion.117), channel_id=1, source_target_pairs={{0,4},{4,0},{1,5},{5,1},{2,6},{6,2},{3,7},{7,3},{8,12},{12,8},{9,1... | collective-permute-start | bytes 393224 | tf_op jit(solution)/shard_map/ppermute | solution.py:28
  21.9 2.6 %collective-permute-start.10 = (f32[8,1,8,128]{3,2,1,0:T(8,128)S(1)}, f32[8,1,8,128]{3,2,1,0:T(8,128)S(1)}, u32[]{:S(2)}, u32[]{:S(2)}) collective-permute-start(f32[8,1,8,128]{3,2,1,0:T(8,128)S(1)} %get-tuple-element.59), channel_id=1, source_target_pairs={{8,0},{9,1},{10,2},{11,3},{12,4},{13,5},{14,6},{15,7},{0,8},{1,9},... | collective-permute-start | bytes 98312 | tf_op jit(solution)/shard_map/ppermute | solution.py:34
  25.9 0.9 collective-permute-done.10
  26.8 2.9 %collective-permute-done.9 = f32[8,1,8,128]{3,2,1,0:T(8,128)S(1)} collective-permute-done((f32[8,1,8,128]{3,2,1,0:T(8,128)S(1)}, f32[8,1,8,128]{3,2,1,0:T(8,128)S(1)}, u32[]{:S(2)}, u32[]{:S(2)}) %collective-permute-start.9) | collective-permute-done | bytes 32800 | tf_op jit(solution)/shard_map/ppermute | solution.py:34
  31.1 2.9 %collective-permute-start.12 = (f32[9,1,8,128]{3,2,1,0:T(8,128)S(1)}, f32[9,1,8,128]{3,2,1,0:T(8,128)S(1)}, u32[]{:S(2)}, u32[]{:S(2)}) collective-permute-start(f32[9,1,8,128]{3,2,1,0:T(8,128)S(1)} %get-tuple-element.46), channel_id=1, source_target_pairs={{8,0},{9,1},{10,2},{11,3},{12,4},{13,5},{14,6},{15,7},{0,8},{1,9},... | collective-permute-start | bytes 110600 | tf_op jit(solution)/shard_map/ppermute | solution.py:34
  34.2 1.2 %collective-permute-done.13 = f32[2,16,8,128]{3,2,1,0:T(8,128)S(1)} collective-permute-done((f32[2,16,8,128]{3,2,1,0:T(8,128)S(1)}, f32[2,16,8,128]{3,2,1,0:T(8,128)S(1)}, u32[]{:S(2)}, u32[]{:S(2)}) %collective-permute-start.13) | collective-permute-done | bytes 131104 | tf_op jit(solution)/shard_map/ppermute | solution.py:28
  35.4 1.4 %collective-permute-start.14 = (f32[2,16,8,128]{3,2,1,0:T(8,128)S(1)}, f32[2,16,8,128]{3,2,1,0:T(8,128)S(1)}, u32[]{:S(2)}, u32[]{:S(2)}) collective-permute-start(f32[2,16,8,128]{3,2,1,0:T(8,128)S(1)} %fusion.101), channel_id=1, source_target_pairs={{0,2},{2,0},{1,3},{3,1},{4,6},{6,4},{5,7},{7,5},{8,10},{10,8},{9,1... | collective-permute-start | bytes 393224 | tf_op jit(solution)/shard_map/ppermute | solution.py:28
  37.6 3.5 %collective-permute-done.14 = f32[2,16,8,128]{3,2,1,0:T(8,128)S(1)} collective-permute-done((f32[2,16,8,128]{3,2,1,0:T(8,128)S(1)}, f32[2,16,8,128]{3,2,1,0:T(8,128)S(1)}, u32[]{:S(2)}, u32[]{:S(2)}) %collective-permute-start.14) | collective-permute-done | bytes 131104 | tf_op jit(solution)/shard_map/ppermute | solution.py:28
  41.4 4.7 %collective-permute-done.15 = f32[2,16,8,128]{3,2,1,0:T(8,128)S(1)} collective-permute-done((f32[2,16,8,128]{3,2,1,0:T(8,128)S(1)}, f32[2,16,8,128]{3,2,1,0:T(8,128)S(1)}, u32[]{:S(2)}, u32[]{:S(2)}) %collective-permute-start.15) | collective-permute-done | bytes 131104 | tf_op jit(solution)/shard_map/ppermute | solution.py:28
  47.6 1.0 collective-permute-done.16
  48.6 1.4 %collective-permute-start.17 = (f32[3,16,8,128]{3,2,1,0:T(8,128)S(1)}, f32[3,16,8,128]{3,2,1,0:T(8,128)S(1)}, u32[]{:S(2)}, u32[]{:S(2)}) collective-permute-start(f32[3,16,8,128]{3,2,1,0:T(8,128)S(1)} %fusion.106), channel_id=1, source_target_pairs={{0,2},{2,0},{1,3},{3,1},{4,6},{6,4},{5,7},{7,5},{8,10},{10,8},{9,1... | collective-permute-start | bytes 589832 | tf_op jit(solution)/shard_map/ppermute | solution.py:28
  50.2 2.8 %collective-permute-start.20 = (f32[9,1,8,128]{3,2,1,0:T(8,128)S(1)}, f32[9,1,8,128]{3,2,1,0:T(8,128)S(1)}, u32[]{:S(2)}, u32[]{:S(2)}) collective-permute-start(f32[9,1,8,128]{3,2,1,0:T(8,128)S(1)} %get-tuple-element.56), channel_id=1, source_target_pairs={{8,0},{9,1},{10,2},{11,3},{12,4},{13,5},{14,6},{15,7},{0,8},{1,9},... | collective-permute-start | bytes 110600 | tf_op jit(solution)/shard_map/ppermute | solution.py:34
  53.1 2.5 %collective-permute-done.17 = f32[3,16,8,128]{3,2,1,0:T(8,128)S(1)} collective-permute-done((f32[3,16,8,128]{3,2,1,0:T(8,128)S(1)}, f32[3,16,8,128]{3,2,1,0:T(8,128)S(1)}, u32[]{:S(2)}, u32[]{:S(2)}) %collective-permute-start.17) | collective-permute-done | bytes 196640 | tf_op jit(solution)/shard_map/ppermute | solution.py:28
  56.8 5.0 %collective-permute-done.18 = f32[3,16,8,128]{3,2,1,0:T(8,128)S(1)} collective-permute-done((f32[3,16,8,128]{3,2,1,0:T(8,128)S(1)}, f32[3,16,8,128]{3,2,1,0:T(8,128)S(1)}, u32[]{:S(2)}, u32[]{:S(2)}) %collective-permute-start.18) | collective-permute-done | bytes 196640 | tf_op jit(solution)/shard_map/ppermute | solution.py:28
  62.0 1.1 multiply_reduce_fusion.5
  63.4 1.0 fusion.10
  65.2 2.8 %collective-permute-start.25 = (f32[9,1,8,128]{3,2,1,0:T(8,128)}, f32[9,1,8,128]{3,2,1,0:T(8,128)}, u32[]{:S(2)}, u32[]{:S(2)}) collective-permute-start(f32[9,1,8,128]{3,2,1,0:T(8,128)} %get-tuple-element.36), channel_id=1, source_target_pairs={{8,0},{9,1},{10,2},{11,3},{12,4},{13,5},{14,6},{15,7},{0,8},{1,9},... | collective-permute-start | bytes 110600 | tf_op jit(solution)/shard_map/ppermute | solution.py:34
  68.1 1.1 fusion.7
  69.2 1.4 %collective-permute-start.22 = (f32[3,16,8,128]{3,2,1,0:T(8,128)S(1)}, f32[3,16,8,128]{3,2,1,0:T(8,128)S(1)}, u32[]{:S(2)}, u32[]{:S(2)}) collective-permute-start(f32[3,16,8,128]{3,2,1,0:T(8,128)S(1)} %fusion.105), channel_id=1, source_target_pairs={{0,2},{2,0},{1,3},{3,1},{4,6},{6,4},{5,7},{7,5},{8,10},{10,8},{9,1... | collective-permute-start | bytes 589832 | tf_op jit(solution)/shard_map/ppermute | solution.py:28
  70.8 5.3 %collective-permute-done.22 = f32[3,16,8,128]{3,2,1,0:T(8,128)S(1)} collective-permute-done((f32[3,16,8,128]{3,2,1,0:T(8,128)S(1)}, f32[3,16,8,128]{3,2,1,0:T(8,128)S(1)}, u32[]{:S(2)}, u32[]{:S(2)}) %collective-permute-start.22) | collective-permute-done | bytes 196640 | tf_op jit(solution)/shard_map/ppermute | solution.py:28
  77.8 30.8 %psum.7 = f32[64]{0:T(128)} all-reduce(f32[64]{0:T(128)S(1)} %multiply_dynamic-update-slice_fusion), channel_id=1, replica_groups=mesh['runs'=2,'space'=16] {'space'}, use_global_device_ids=true, to_apply=%region_14.15 | all-reduce | flops 64 | bytes 512 | tf_op jit(solution)/shard_map/psum | solution.py:160
  108.7 2.0 %fusion.5 = f32[9,16,8,128]{3,2,1,0:T(8,128)S(1)} fusion(f32[1,16,8,128]{3,2,1,0:T(8,128)S(1)} %get-tuple-element.25, f32[9,1,8,128]{3,2,1,0:T(8,128)} %collective-permute-done.25, f32[8,16,8,128]{3,2,1,0:T(8,128)S(1)} %broadcast_multiply_fusion, f32[9,1,8,128]{3,2,1,0:T(8,128)} %collective-permute-done.24, f32[9,16,7,128]{3,2,1,0:T(8,128)} %get-tuple-element.32, ...), kind=kLoop, calls=%fused_computation.54 | loop fusion | flops 2359296 | bytes 3612672 | tf_op jit(solution)/shard_map/add | solution.py:79
  110.7 1.0 add.319
  112.7 1.4 %fusion.54 = f32[1,8,16,8,128]{4,3,2,1,0:T(8,128)} fusion(f32[8,16,8,128]{3,2,1,0:T(8,128)S(1)} %get-tuple-element.17, f32[8,16,8,128]{3,2,1,0:T(8,128)S(1)} %get-tuple-element.20, f32[9,16,8,128]{3,2,1,0:T(8,128)S(1)} %fusion.5, f32[16,8,128]{2,1,0:T(8,128)S(1)} %get-tuple-element.22, f32[16,8,128]{2,1,0:T(8,128)S(1)} %get-tuple-element.21, ...), kind=kLoop, calls=%fused_computation.127 | loop fusion | flops 3801088 | bytes 2490432 | tf_op jit(solution)/shard_map/broadcast_in_dim | solution.py:162
  (107 shorter events, 16.0 us)
Async XLA Ops:
  0.6 12.2 %copy-start.9 = (f32[1,8,16,8,128]{4,3,2,1,0:T(8,128)S(1)}, f32[1,8,16,8,128]{4,3,2,1,0:T(8,128)}, u32[]{:S(2)}) copy-start(f32[1,8,16,8,128]{4,3,2,1,0:T(8,128)} %param.6) | copy-start | bytes 1572868
  0.6 2.1 %collective-permute-start.3 = (s32[2,8,128]{2,1,0:T(8,128)}, s32[2,8,128]{2,1,0:T(8,128)S(1)}, u32[]{:S(2)}, u32[]{:S(2)}) collective-permute-start(s32[2,8,128]{2,1,0:T(8,128)} %param.7), channel_id=1, source_target_pairs={{0,1},{1,0},{2,3},{3,2},{4,5},{5,4},{6,7},{7,6},{8,9},{9,8},{10,11... | collective-permute-start | bytes 24584 | tf_op jit(solution)/shard_map/ppermute | solution.py:28
  1.9 4.5 %collective-permute-start = (f32[2,2,8,128]{3,2,1,0:T(8,128)S(1)}, f32[2,2,8,128]{3,2,1,0:T(8,128)S(1)}, u32[]{:S(2)}, u32[]{:S(2)}) collective-permute-start(f32[2,2,8,128]{3,2,1,0:T(8,128)S(1)} %pad_maximum_fusion.21), channel_id=1, source_target_pairs={{0,1},{1,0},{2,3},{3,2},{4,5},{5,4},{6,7},{7,6},{8,9},{9,8},{10,11... | collective-permute-start | bytes 49160 | tf_op jit(solution)/shard_map/ppermute | solution.py:28
  3.5 4.6 %collective-permute-start.4 = (s32[4,8,128]{2,1,0:T(8,128)S(1)}, s32[4,8,128]{2,1,0:T(8,128)S(1)}, u32[]{:S(2)}, u32[]{:S(2)}) collective-permute-start(s32[4,8,128]{2,1,0:T(8,128)S(1)} %add_select_fusion.2), channel_id=1, source_target_pairs={{0,2},{2,0},{1,3},{3,1},{4,6},{6,4},{5,7},{7,5},{8,10},{10,8},{9,1... | collective-permute-start | bytes 49160 | tf_op jit(solution)/shard_map/ppermute | solution.py:28
  7.2 3.9 %collective-permute-start.1 = (f32[2,4,8,128]{3,2,1,0:T(8,128)S(1)}, f32[2,4,8,128]{3,2,1,0:T(8,128)S(1)}, u32[]{:S(2)}, u32[]{:S(2)}) collective-permute-start(f32[2,4,8,128]{3,2,1,0:T(8,128)S(1)} %maximum_select_fusion.2), channel_id=1, source_target_pairs={{0,2},{2,0},{1,3},{3,1},{4,6},{6,4},{5,7},{7,5},{8,10},{10,8},{9,1... | collective-permute-start | bytes 98312 | tf_op jit(solution)/shard_map/ppermute | solution.py:28
  8.1 4.6 %collective-permute-start.5 = (s32[8,8,128]{2,1,0:T(8,128)S(1)}, s32[8,8,128]{2,1,0:T(8,128)S(1)}, u32[]{:S(2)}, u32[]{:S(2)}) collective-permute-start(s32[8,8,128]{2,1,0:T(8,128)S(1)} %add_select_fusion.1), channel_id=1, source_target_pairs={{0,4},{4,0},{1,5},{5,1},{2,6},{6,2},{3,7},{7,3},{8,12},{12,8},{9,1... | collective-permute-start | bytes 98312 | tf_op jit(solution)/shard_map/ppermute | solution.py:28
  11.1 13.8 %collective-permute-start.2 = (f32[2,8,8,128]{3,2,1,0:T(8,128)S(1)}, f32[2,8,8,128]{3,2,1,0:T(8,128)S(1)}, u32[]{:S(2)}, u32[]{:S(2)}) collective-permute-start(f32[2,8,8,128]{3,2,1,0:T(8,128)S(1)} %maximum_select_fusion.1), channel_id=1, source_target_pairs={{0,4},{4,0},{1,5},{5,1},{2,6},{6,2},{3,7},{7,3},{8,12},{12,8},{9,1... | collective-permute-start | bytes 196616 | tf_op jit(solution)/shard_map/ppermute | solution.py:28
  13.3 1.4 %collective-permute-start.6 = (f32[2,16,8,128]{3,2,1,0:T(8,128)S(1)}, f32[2,16,8,128]{3,2,1,0:T(8,128)S(1)}, u32[]{:S(2)}, u32[]{:S(2)}) collective-permute-start(f32[2,16,8,128]{3,2,1,0:T(8,128)S(1)} %pad_maximum_fusion.19), channel_id=1, source_target_pairs={{0,1},{1,0},{2,3},{3,2},{4,5},{5,4},{6,7},{7,6},{8,9},{9,8},{10,11... | collective-permute-start | bytes 393224 | tf_op jit(solution)/shard_map/ppermute | solution.py:28
  14.7 5.6 %collective-permute-start.7 = (f32[2,16,8,128]{3,2,1,0:T(8,128)S(1)}, f32[2,16,8,128]{3,2,1,0:T(8,128)S(1)}, u32[]{:S(2)}, u32[]{:S(2)}) collective-permute-start(f32[2,16,8,128]{3,2,1,0:T(8,128)S(1)} %fusion.102), channel_id=1, source_target_pairs={{0,2},{2,0},{1,3},{3,1},{4,6},{6,4},{5,7},{7,5},{8,10},{10,8},{9,1... | collective-permute-start | bytes 393224 | tf_op jit(solution)/shard_map/ppermute | solution.py:28
  20.4 5.4 %collective-permute-start.8 = (f32[2,16,8,128]{3,2,1,0:T(8,128)S(1)}, f32[2,16,8,128]{3,2,1,0:T(8,128)S(1)}, u32[]{:S(2)}, u32[]{:S(2)}) collective-permute-start(f32[2,16,8,128]{3,2,1,0:T(8,128)S(1)} %fusion.117), channel_id=1, source_target_pairs={{0,4},{4,0},{1,5},{5,1},{2,6},{6,2},{3,7},{7,3},{8,12},{12,8},{9,1... | collective-permute-start | bytes 393224 | tf_op jit(solution)/shard_map/ppermute | solution.py:28
  21.9 4.8 %collective-permute-start.10 = (f32[8,1,8,128]{3,2,1,0:T(8,128)S(1)}, f32[8,1,8,128]{3,2,1,0:T(8,128)S(1)}, u32[]{:S(2)}, u32[]{:S(2)}) collective-permute-start(f32[8,1,8,128]{3,2,1,0:T(8,128)S(1)} %get-tuple-element.59), channel_id=1, source_target_pairs={{8,0},{9,1},{10,2},{11,3},{12,4},{13,5},{14,6},{15,7},{0,8},{1,9},... | collective-permute-start | bytes 98312 | tf_op jit(solution)/shard_map/ppermute | solution.py:34
  24.5 5.1 %collective-permute-start.9 = (f32[8,1,8,128]{3,2,1,0:T(8,128)S(1)}, f32[8,1,8,128]{3,2,1,0:T(8,128)S(1)}, u32[]{:S(2)}, u32[]{:S(2)}) collective-permute-start(f32[8,1,8,128]{3,2,1,0:T(8,128)S(1)} %get-tuple-element.58), channel_id=1, source_target_pairs={{8,0},{9,1},{10,2},{11,3},{12,4},{13,5},{14,6},{15,7},{0,8},{1,9},... | collective-permute-start | bytes 98312 | tf_op jit(solution)/shard_map/ppermute | solution.py:34
  25.8 4.7 %copy-start.7 = (f32[16,8,128]{2,1,0:T(8,128)}, f32[16,8,128]{2,1,0:T(8,128)S(1)}, u32[]{:S(2)}) copy-start(f32[16,8,128]{2,1,0:T(8,128)S(1)} %get-tuple-element.83) | copy-start | bytes 196612
  25.8 36.1 %copy-start.1 = (f32[16,8,128]{2,1,0:T(8,128)}, f32[16,8,128]{2,1,0:T(8,128)S(1)}, u32[]{:S(2)}) copy-start(f32[16,8,128]{2,1,0:T(8,128)S(1)} %get-tuple-element.81) | copy-start | bytes 196612
  25.9 36.1 %copy-start.3 = (f32[16,8,128]{2,1,0:T(8,128)}, f32[16,8,128]{2,1,0:T(8,128)S(1)}, u32[]{:S(2)}) copy-start(f32[16,8,128]{2,1,0:T(8,128)S(1)} %get-tuple-element.82) | copy-start | bytes 196612
  25.9 36.1 %copy-start.5 = (f32[16,8,128]{2,1,0:T(8,128)}, f32[16,8,128]{2,1,0:T(8,128)S(1)}, u32[]{:S(2)}) copy-start(f32[16,8,128]{2,1,0:T(8,128)S(1)} %get-tuple-element.84) | copy-start | bytes 196612
  31.0 6.0 %collective-permute-start.11 = (f32[9,1,8,128]{3,2,1,0:T(8,128)S(1)}, f32[9,1,8,128]{3,2,1,0:T(8,128)S(1)}, u32[]{:S(2)}, u32[]{:S(2)}) collective-permute-start(f32[9,1,8,128]{3,2,1,0:T(8,128)S(1)} %get-tuple-element.45), channel_id=1, source_target_pairs={{8,0},{9,1},{10,2},{11,3},{12,4},{13,5},{14,6},{15,7},{0,8},{1,9},... | collective-permute-start | bytes 110600 | tf_op jit(solution)/shard_map/ppermute | solution.py:34
  31.1 5.9 %collective-permute-start.12 = (f32[9,1,8,128]{3,2,1,0:T(8,128)S(1)}, f32[9,1,8,128]{3,2,1,0:T(8,128)S(1)}, u32[]{:S(2)}, u32[]{:S(2)}) collective-permute-start(f32[9,1,8,128]{3,2,1,0:T(8,128)S(1)} %get-tuple-element.46), channel_id=1, source_target_pairs={{8,0},{9,1},{10,2},{11,3},{12,4},{13,5},{14,6},{15,7},{0,8},{1,9},... | collective-permute-start | bytes 110600 | tf_op jit(solution)/shard_map/ppermute | solution.py:34
  34.0 1.4 %collective-permute-start.13 = (f32[2,16,8,128]{3,2,1,0:T(8,128)S(1)}, f32[2,16,8,128]{3,2,1,0:T(8,128)S(1)}, u32[]{:S(2)}, u32[]{:S(2)}) collective-permute-start(f32[2,16,8,128]{3,2,1,0:T(8,128)S(1)} %pad_maximum_fusion.20), channel_id=1, source_target_pairs={{0,1},{1,0},{2,3},{3,2},{4,5},{5,4},{6,7},{7,6},{8,9},{9,8},{10,11... | collective-permute-start | bytes 393224 | tf_op jit(solution)/shard_map/ppermute | solution.py:28
  35.4 5.6 %collective-permute-start.14 = (f32[2,16,8,128]{3,2,1,0:T(8,128)S(1)}, f32[2,16,8,128]{3,2,1,0:T(8,128)S(1)}, u32[]{:S(2)}, u32[]{:S(2)}) collective-permute-start(f32[2,16,8,128]{3,2,1,0:T(8,128)S(1)} %fusion.101), channel_id=1, source_target_pairs={{0,2},{2,0},{1,3},{3,1},{4,6},{6,4},{5,7},{7,5},{8,10},{10,8},{9,1... | collective-permute-start | bytes 393224 | tf_op jit(solution)/shard_map/ppermute | solution.py:28
  41.1 5.1 %copy-start = (f32[1,8,16,8,128]{4,3,2,1,0:T(8,128)S(1)}, f32[1,8,16,8,128]{4,3,2,1,0:T(8,128)}, u32[]{:S(2)}) copy-start(f32[1,8,16,8,128]{4,3,2,1,0:T(8,128)} %param.10) | copy-start | bytes 1572868
  41.1 5.0 %collective-permute-start.15 = (f32[2,16,8,128]{3,2,1,0:T(8,128)S(1)}, f32[2,16,8,128]{3,2,1,0:T(8,128)S(1)}, u32[]{:S(2)}, u32[]{:S(2)}) collective-permute-start(f32[2,16,8,128]{3,2,1,0:T(8,128)S(1)} %fusion.116), channel_id=1, source_target_pairs={{0,4},{4,0},{1,5},{5,1},{2,6},{6,2},{3,7},{7,3},{8,12},{12,8},{9,1... | collective-permute-start | bytes 393224 | tf_op jit(solution)/shard_map/ppermute | solution.py:28
  47.1 1.5 %collective-permute-start.16 = (f32[3,16,8,128]{3,2,1,0:T(8,128)S(1)}, f32[3,16,8,128]{3,2,1,0:T(8,128)S(1)}, u32[]{:S(2)}, u32[]{:S(2)}) collective-permute-start(f32[3,16,8,128]{3,2,1,0:T(8,128)S(1)} %pad_maximum_fusion.17), channel_id=1, source_target_pairs={{0,1},{1,0},{2,3},{3,2},{4,5},{5,4},{6,7},{7,6},{8,9},{9,8},{10,11... | collective-permute-start | bytes 589832 | tf_op jit(solution)/shard_map/ppermute | solution.py:28
  48.6 7.0 %collective-permute-start.17 = (f32[3,16,8,128]{3,2,1,0:T(8,128)S(1)}, f32[3,16,8,128]{3,2,1,0:T(8,128)S(1)}, u32[]{:S(2)}, u32[]{:S(2)}) collective-permute-start(f32[3,16,8,128]{3,2,1,0:T(8,128)S(1)} %fusion.106), channel_id=1, source_target_pairs={{0,2},{2,0},{1,3},{3,1},{4,6},{6,4},{5,7},{7,5},{8,10},{10,8},{9,1... | collective-permute-start | bytes 589832 | tf_op jit(solution)/shard_map/ppermute | solution.py:28
  50.1 6.0 %collective-permute-start.19 = (f32[9,1,8,128]{3,2,1,0:T(8,128)S(1)}, f32[9,1,8,128]{3,2,1,0:T(8,128)S(1)}, u32[]{:S(2)}, u32[]{:S(2)}) collective-permute-start(f32[9,1,8,128]{3,2,1,0:T(8,128)S(1)} %get-tuple-element.55), channel_id=1, source_target_pairs={{8,0},{9,1},{10,2},{11,3},{12,4},{13,5},{14,6},{15,7},{0,8},{1,9},... | collective-permute-start | bytes 110600 | tf_op jit(solution)/shard_map/ppermute | solution.py:34
  50.2 6.1 %collective-permute-start.20 = (f32[9,1,8,128]{3,2,1,0:T(8,128)S(1)}, f32[9,1,8,128]{3,2,1,0:T(8,128)S(1)}, u32[]{:S(2)}, u32[]{:S(2)}) collective-permute-start(f32[9,1,8,128]{3,2,1,0:T(8,128)S(1)} %get-tuple-element.56), channel_id=1, source_target_pairs={{8,0},{9,1},{10,2},{11,3},{12,4},{13,5},{14,6},{15,7},{0,8},{1,9},... | collective-permute-start | bytes 110600 | tf_op jit(solution)/shard_map/ppermute | solution.py:34
  55.7 6.2 %collective-permute-start.18 = (f32[3,16,8,128]{3,2,1,0:T(8,128)S(1)}, f32[3,16,8,128]{3,2,1,0:T(8,128)S(1)}, u32[]{:S(2)}, u32[]{:S(2)}) collective-permute-start(f32[3,16,8,128]{3,2,1,0:T(8,128)S(1)} %fusion.115), channel_id=1, source_target_pairs={{0,4},{4,0},{1,5},{5,1},{2,6},{6,2},{3,7},{7,3},{8,12},{12,8},{9,1... | collective-permute-start | bytes 589832 | tf_op jit(solution)/shard_map/ppermute | solution.py:28
  64.4 4.8 %collective-permute-start.21 = (f32[3,16,8,128]{3,2,1,0:T(8,128)S(1)}, f32[3,16,8,128]{3,2,1,0:T(8,128)S(1)}, u32[]{:S(2)}, u32[]{:S(2)}) collective-permute-start(f32[3,16,8,128]{3,2,1,0:T(8,128)S(1)} %pad_maximum_fusion.18), channel_id=1, source_target_pairs={{0,1},{1,0},{2,3},{3,2},{4,5},{5,4},{6,7},{7,6},{8,9},{9,8},{10,11... | collective-permute-start | bytes 589832 | tf_op jit(solution)/shard_map/ppermute | solution.py:28
  65.1 43.5 %collective-permute-start.24 = (f32[9,1,8,128]{3,2,1,0:T(8,128)}, f32[9,1,8,128]{3,2,1,0:T(8,128)}, u32[]{:S(2)}, u32[]{:S(2)}) collective-permute-start(f32[9,1,8,128]{3,2,1,0:T(8,128)} %get-tuple-element.35), channel_id=1, source_target_pairs={{8,0},{9,1},{10,2},{11,3},{12,4},{13,5},{14,6},{15,7},{0,8},{1,9},... | collective-permute-start | bytes 110600 | tf_op jit(solution)/shard_map/ppermute | solution.py:34
  65.2 43.4 %collective-permute-start.25 = (f32[9,1,8,128]{3,2,1,0:T(8,128)}, f32[9,1,8,128]{3,2,1,0:T(8,128)}, u32[]{:S(2)}, u32[]{:S(2)}) collective-permute-start(f32[9,1,8,128]{3,2,1,0:T(8,128)} %get-tuple-element.36), channel_id=1, source_target_pairs={{8,0},{9,1},{10,2},{11,3},{12,4},{13,5},{14,6},{15,7},{0,8},{1,9},... | collective-permute-start | bytes 110600 | tf_op jit(solution)/shard_map/ppermute | solution.py:34
  69.2 6.8 %collective-permute-start.22 = (f32[3,16,8,128]{3,2,1,0:T(8,128)S(1)}, f32[3,16,8,128]{3,2,1,0:T(8,128)S(1)}, u32[]{:S(2)}, u32[]{:S(2)}) collective-permute-start(f32[3,16,8,128]{3,2,1,0:T(8,128)S(1)} %fusion.105), channel_id=1, source_target_pairs={{0,2},{2,0},{1,3},{3,1},{4,6},{6,4},{5,7},{7,5},{8,10},{10,8},{9,1... | collective-permute-start | bytes 589832 | tf_op jit(solution)/shard_map/ppermute | solution.py:28
  76.8 33.9 %collective-permute-start.23 = (f32[3,16,8,128]{3,2,1,0:T(8,128)}, f32[3,16,8,128]{3,2,1,0:T(8,128)}, u32[]{:S(2)}, u32[]{:S(2)}) collective-permute-start(f32[3,16,8,128]{3,2,1,0:T(8,128)} %fusion.114), channel_id=1, source_target_pairs={{0,4},{4,0},{1,5},{5,1},{2,6},{6,2},{3,7},{7,3},{8,12},{12,8},{9,1... | collective-permute-start | bytes 589832 | tf_op jit(solution)/shard_map/ppermute | solution.py:28
  (4 other events, 3.5 us)
where the time goes:
time: 115 us
  waiting for transfers between devices  35 us (30%)
  blocking collectives  30.8 us (27%)
  starting transfers between devices  27.6 us (24%)
  other arithmetic  18.7 us (16%)
  local copies, waits for them, and re-layouts  1.46 us (1%)
    ppermute x18, waiting for transfers between devices, swapped(): return lax.ppermute(block, axis, route)  31.1 us
    psum x1, blocking collectives, body(): mobility_gradient = lax.psum(placed, 'space')  30.8 us
    ppermute x18, starting transfers between devices, swapped(): return lax.ppermute(block, axis, route)  15.9 us
    ppermute x8, starting transfers between devices, from_behind(): return lax.ppermute(block, axis, route)  11.8 us
    concatenate x10, other arithmetic, backward_step(): stacked = jnp.concatenate([weighted, adj_conc[None]], 0)  4.37 us
    ppermute x8, waiting for transfers between devices, from_behind(): return lax.ppermute(block, axis, route)  3.97 us
    add x3, other arithmetic, laplace_rows(): return result + jnp.roll(middle, 1, 3) + jnp.roll(middle, -1, 3)  3.18 us
  transfers between devices with their start and end apart: 26, of which 15 were waited for; matrix products, arithmetic and copies ran while one was open for 10% of the time, Pallas kernels for 0%

commit v1 on v0

v1 whole, which is shorter than its diff:
```python
import functools

import jax
import jax.numpy as jnp
from jax import lax
from jax.experimental import pallas as pl
from jax.experimental.pallas import tpu as pltpu
from jax.sharding import PartitionSpec as P

P_SIZE = 64
GROUPS = 8

time_step = 0.1
gradient_coef = 0.75
coupling = 1.5
chem_height = 2.5
alpha_level = 0.2
beta_level = 0.8
solute_mobility = 0.3
epsilon = 1e-05

MESH = pl.DeviceIdType.MESH
CUBIC = 1.0 - 2.0 * coupling
GAP = beta_level - alpha_level
BETA_GROUP = GROUPS // 2

LABELS, SUM_A, COEF_A, SUM_B, COEF_B, SUM_C, COEF_C, MOBILITY = range(8)
PHASE_RIM, ADJ_RIM, BAR_RIM, ADJ_RING, POT_RING, BAR_RING = range(6)


def turn(x):
    last = x.ndim - 1
    lanes, rows = x.shape[-1], x.shape[-2]
    across = pltpu.roll(x, 1, last) + pltpu.roll(x, lanes - 1, last)
    return across + (pltpu.roll(x, 1, last - 1) + pltpu.roll(x, rows - 1, last - 1))


def curve(ref, layer):
    middle = ref[:, layer + 1]
    return (ref[:, layer] + ref[:, layer + 2] - 6.0 * middle) + turn(middle)


def curve_cells(ref):
    middle = ref[1:-1]
    return (ref[:-2] + ref[2:] - 6.0 * middle) + turn(middle)


def kernel(
    slabs, noise_ref, labels_ref, solute_ref, mobility_ref, adj_ref, adjc_ref,
    grad_ref, solgrad_ref, mobgrad_ref,
    phi, lam, bar, phi1, drive, pre, rate_buf, lab, conc, adjc, pot, adjc1,
    sum_a, got_a, put_a, coef_a, sum_b, got_b, put_b, coef_b, sum_c, got_c, put_c, coef_c,
    mob_mine, mob_slabs, mob_all,
    load_sem, out_sem, send_sem, recv_sem, rim_send, rim_recv, mob_send, mob_recv,
):
    orders, layers = noise_ref.shape[0], noise_ref.shape[1]
    sub = layers // GROUPS
    place = lax.axis_index("space")
    count = slabs * GROUPS
    group = lax.rem(place, GROUPS)
    slab = lax.div(place, GROUPS)
    base = slab * GROUPS
    after, before = lax.rem(place + 1, count), lax.rem(place + count - 1, count)
    above, below = lax.rem(place + GROUPS, count), lax.rem(place + count - GROUPS, count)

    def peer(j):
        return lax.rem(group + j, GROUPS)

    def other_slab(s):
        return lax.rem(slab + s, slabs) * GROUPS + group

    barrier = pltpu.get_barrier_semaphore()
    for j in range(1, GROUPS):
        pl.semaphore_signal(barrier, inc=1, device_id={"space": base + peer(j)}, device_id_type=MESH)
    for s in range(1, slabs):
        pl.semaphore_signal(barrier, inc=1, device_id={"space": other_slab(s)}, device_id_type=MESH)
    for device in (after, before):
        pl.semaphore_signal(barrier, inc=1, device_id={"space": device}, device_id_type=MESH)

    load_labels = pltpu.make_async_copy(labels_ref, lab.at[group], load_sem.at[0])
    load_noise = pltpu.make_async_copy(noise_ref, phi.at[:, pl.ds(1, layers)], load_sem.at[1])
    load_adjc = pltpu.make_async_copy(adjc_ref, adjc.at[pl.ds(1, sub)], load_sem.at[2])
    load_solute = pltpu.make_async_copy(solute_ref, conc, load_sem.at[3])
    load_adj = pltpu.make_async_copy(adj_ref, lam.at[:, pl.ds(1, layers)], load_sem.at[4])
    for load in (load_labels, load_noise, load_adjc, load_solute, load_adj):
        load.start()
    for i in range(orders):
        rate_buf[i] = jnp.full(rate_buf.shape[1:], time_step * mobility_ref[group * orders + i], jnp.float32)

    pl.semaphore_wait(barrier, GROUPS - 1 + slabs - 1 + 2)

    def to_peer(kind, src, dst, p):
        return pltpu.make_async_remote_copy(
            src_ref=src, dst_ref=dst, send_sem=send_sem.at[kind, p], recv_sem=recv_sem.at[kind, group],
            device_id={"space": base + p}, device_id_type=MESH,
        )

    def arrived(kind, dst, p):
        pltpu.make_async_remote_copy(
            src_ref=dst, dst_ref=dst, send_sem=send_sem.at[kind, p], recv_sem=recv_sem.at[kind, p],
            device_id={"space": base + p}, device_id_type=MESH,
        ).wait_recv()

    def sent(kind, src, p):
        pltpu.make_async_remote_copy(
            src_ref=src, dst_ref=src, send_sem=send_sem.at[kind, p], recv_sem=recv_sem.at[kind, p],
            device_id={"space": base + p}, device_id_type=MESH,
        ).wait_send()

    def over_peers(act):
        def run(j, carry):
            act(peer(j))
            return carry

        lax.fori_loop(1, GROUPS, run, 0)

    def rim_copy(kind, side, src, dst, device):
        return pltpu.make_async_remote_copy(
            src_ref=src, dst_ref=dst, send_sem=rim_send.at[kind, side], recv_sem=rim_recv.at[kind, side],
            device_id={"space": device}, device_id_type=MESH,
        )

    def rims_of(kind, src, ref, offset):
        last = layers + 1
        return (
            rim_copy(kind, 0, src.at[:, layers - 1 + offset], ref.at[:, 0], above),
            rim_copy(kind, 1, src.at[:, offset], ref.at[:, last], below),
        )

    def ring_of(kind, src, ref, offset):
        return (
            rim_copy(kind, 0, src.at[sub - 1 + offset], ref.at[0], after),
            rim_copy(kind, 1, src.at[offset], ref.at[sub + 1], before),
        )

    over_peers(lambda p: to_peer(LABELS, labels_ref, lab.at[group], p).start())
    adj_ring = ring_of(ADJ_RING, adjc_ref, adjc, 0)
    adj_rim = rims_of(ADJ_RIM, adj_ref, lam, 0)
    for copy in adj_ring:
        copy.start()

    def start_chunk(p):
        for k in range(sub):
            z = p * sub + k
            ids = group * orders + lax.broadcasted_iota(jnp.int32, rate_buf.shape, 0)
            field = phi[:, z + 1] + jnp.where(lab[p, k][None] == ids, 0.5, 0.0)
            phi[:, z + 1] = field
            sum_a[p, k] = jnp.sum(field * field, axis=0)

    load_labels.wait()
    load_noise.wait()
    start_chunk(group)
    got_a[group] = sum_a[group]

    def start_peer(p):
        arrived(LABELS, lab.at[p], p)
        start_chunk(p)
        to_peer(SUM_A, sum_a.at[p], got_a.at[group], p).start()

    over_peers(start_peer)
    phase_rim = rims_of(PHASE_RIM, phi, phi, 1)
    for copy in phase_rim + adj_rim:
        copy.start()

    def local_drive(z):
        field = phi[:, z + 1]
        drive[:, z] = CUBIC * field * field * field - gradient_coef * curve(phi, z)

    def over_inner(act):
        def run(z, carry):
            act(z)
            return carry

        lax.fori_loop(1, layers - 1, run, 0)

    over_inner(local_drive)
    load_adjc.wait()
    load_solute.wait()
    load_adj.wait()
    for copy in adj_ring:
        copy.wait_recv()

    def total_of(parts):
        low, high = parts[0], parts[BETA_GROUP]
        for g in range(1, BETA_GROUP):
            low = low + parts[g]
            high = high + parts[BETA_GROUP + g]
        return low + high, high

    def state_of(squares, beta_squares, c):
        inverse = 1.0 / (squares + epsilon)
        share = beta_squares * inverse
        slope = chem_height * ((c - beta_level) ** 2 - (c - alpha_level) ** 2)
        pull = 2.0 * slope * inverse
        plain = 2.0 * coupling * squares - 1.0 - pull * share
        return inverse, share, pull, plain

    def adjoint_of(state, moment, beta_moment, pot_bar):
        inverse, share, pull, _ = state
        scaled = pull * inverse
        pot_part = (2.0 * chem_height * GAP) * inverse * pot_bar
        all_bar = 2.0 * coupling * moment - scaled * (beta_moment - 2.0 * share * moment) + share * pot_part
        beta_bar = -scaled * moment - pot_part
        c_bar = (-4.0 * chem_height * GAP) * inverse * (beta_moment - share * moment) + 2.0 * chem_height * pot_bar
        return 2.0 * all_bar, 2.0 * (all_bar + beta_bar), c_bar

    over_peers(lambda p: arrived(SUM_A, got_a.at[p], p))
    state_a = state_of(*total_of(got_a), conc[...])
    put_a[0] = state_a[3]
    put_a[1] = state_a[3] + state_a[2]
    over_peers(lambda p: to_peer(COEF_A, put_a.at[lax.div(p, BETA_GROUP)], coef_a.at[group], p).start())
    coef_a[group] = put_a[lax.div(group, BETA_GROUP)]
    pot[1 : sub + 1] = 2.0 * chem_height * (conc[...] - alpha_level - state_a[1] * GAP)
    pot_ring = ring_of(POT_RING, pot, pot, 1)
    for copy in pot_ring:
        copy.start()

    for copy in phase_rim:
        copy.wait_recv()
    local_drive(0)
    local_drive(layers - 1)

    def step_chunk(p):
        for k in range(sub):
            z = p * sub + k
            field = phi[:, z + 1]
            full = drive[:, z] + field * coef_a[p, k][None]
            drive[:, z] = full
            rate = rate_buf[...]
            following = field - rate * full
            phi1[:, z] = following
            sum_b[p, 0, k] = jnp.sum(following * following, axis=0)
            sum_b[p, 1, k] = -jnp.sum(rate * lam[:, z + 1] * following, axis=0)

    step_chunk(group)
    got_b[group] = sum_b[group]

    def step_peer(p):
        arrived(COEF_A, coef_a.at[p], p)
        step_chunk(p)
        to_peer(SUM_B, sum_b.at[p], got_b.at[group], p).start()

    over_peers(step_peer)

    def local_bar(z, moved):
        adj, field, rate = lam[:, z + 1], phi1[:, z], rate_buf[...]
        curved = gradient_coef * curve(lam, z)
        squared = field * field
        pre[:, z] = adj + rate * (curved - (3.0 * CUBIC) * squared * adj)
        return moved + field * (CUBIC * squared * adj - curved)

    moved = lax.fori_loop(1, layers - 1, local_bar, jnp.zeros(rate_buf.shape, jnp.float32))

    pot_bar_b = (time_step * solute_mobility) * curve_cells(adjc)
    for copy in pot_ring:
        copy.wait_recv()
    conc1 = conc[...] + (time_step * solute_mobility) * curve_cells(pot)
    over_peers(lambda p: arrived(SUM_B, got_b.at[p], p))
    state_b = state_of(*total_of([got_b[g, 0] for g in range(GROUPS)]), conc1)
    plain_b, beta_b, c_bar_b = adjoint_of(
        state_b, *total_of([got_b[g, 1] for g in range(GROUPS)]), pot_bar_b
    )
    put_b[0, 0] = state_b[3]
    put_b[0, 1] = plain_b
    put_b[1, 0] = state_b[3] + state_b[2]
    put_b[1, 1] = beta_b
    over_peers(lambda p: to_peer(COEF_B, put_b.at[lax.div(p, BETA_GROUP)], coef_b.at[group], p).start())
    coef_b[group] = put_b[lax.div(group, BETA_GROUP)]
    adjc1[1 : sub + 1] = adjc[1 : sub + 1] + c_bar_b
    bar_ring = ring_of(BAR_RING, adjc1, adjc1, 1)
    for copy in bar_ring:
        copy.start()

    for copy in adj_rim:
        copy.wait_recv()
    moved = local_bar(0, moved)
    moved = local_bar(layers - 1, moved)

    def bar_chunk(p, moved):
        for k in range(sub):
            z = p * sub + k
            adj, field, rate = lam[:, z + 1], phi1[:, z], rate_buf[...]
            scaled = adj * coef_b[p, 0, k][None]
            full = pre[:, z] + field * coef_b[p, 1, k][None] - rate * scaled
            bar[:, z + 1] = full
            sum_c[p, k] = -jnp.sum(rate * full * phi[:, z + 1], axis=0)
            moved = moved + (field * scaled + full * drive[:, z])
        return moved

    moved = bar_chunk(group, moved)
    got_c[group] = sum_c[group]

    def bar_peer(j, moved):
        p = peer(j)
        arrived(COEF_B, coef_b.at[p], p)
        moved = bar_chunk(p, moved)
        to_peer(SUM_C, sum_c.at[p], got_c.at[group], p).start()
        return moved

    moved = lax.fori_loop(1, GROUPS, bar_peer, moved)
    bar_rim = rims_of(BAR_RIM, bar, bar, 1)
    for copy in bar_rim:
        copy.start()
    mob_mine[...] = -time_step * jnp.sum(moved, axis=1)
    mob_copies = [
        pltpu.make_async_remote_copy(
            src_ref=mob_mine, dst_ref=mob_slabs.at[s - 1], send_sem=mob_send.at[s - 1], recv_sem=mob_recv.at[s - 1],
            device_id={"space": other_slab(s)}, device_id_type=MESH,
        )
        for s in range(1, slabs)
    ]
    for copy in mob_copies:
        copy.start()

    def local_grad(z):
        full, field, rate = bar[:, z + 1], phi[:, z + 1], rate_buf[...]
        p, k = z // sub, z % sub
        slope = coef_a[p, k][None] + (3.0 * CUBIC) * field * field
        pre[:, z] = full + rate * (gradient_coef * curve(bar, z) - full * slope)

    over_inner(local_grad)
    for copy in bar_ring:
        copy.wait_recv()
    pot_bar_a = (time_step * solute_mobility) * curve_cells(adjc1)
    over_peers(lambda p: arrived(SUM_C, got_c.at[p], p))
    plain_c, beta_c, c_bar_a = adjoint_of(state_a, *total_of(got_c), pot_bar_a)
    put_c[0] = plain_c
    put_c[1] = beta_c
    over_peers(lambda p: to_peer(COEF_C, put_c.at[lax.div(p, BETA_GROUP)], coef_c.at[group], p).start())
    coef_c[group] = put_c[lax.div(group, BETA_GROUP)]
    solgrad_ref[...] = adjc1[1 : sub + 1] + c_bar_a

    for copy in mob_copies:
        copy.wait_recv()
    whole = mob_mine[...]
    for s in range(1, slabs):
        whole = whole + mob_slabs[s - 1]
    mob_all[group] = whole
    over_peers(lambda p: to_peer(MOBILITY, mob_all.at[group], mob_all.at[group], p).start())

    for copy in bar_rim:
        copy.wait_recv()
    local_grad(0)
    local_grad(layers - 1)

    def store(p):
        rows = pl.ds(p * sub, sub)
        return pltpu.make_async_copy(pre.at[:, rows], grad_ref.at[:, rows], out_sem.at[p])

    def grad_chunk(p):
        for k in range(sub):
            z = p * sub + k
            pre[:, z] = pre[:, z] + phi[:, z + 1] * coef_c[p, k][None]
        store(p).start()

    grad_chunk(group)

    def grad_peer(p):
        arrived(COEF_C, coef_c.at[p], p)
        grad_chunk(p)

    over_peers(grad_peer)
    over_peers(lambda p: arrived(MOBILITY, mob_all.at[p], p))
    table = mob_all[...].reshape(GROUPS * orders, mob_all.shape[-1])
    mobgrad_ref[...] = jnp.sum(table.T, axis=0, keepdims=True)

    def finish(p):
        sent(LABELS, labels_ref, p)
        sent(SUM_A, sum_a.at[p], p)
        sent(COEF_A, put_a.at[0], p)
        sent(SUM_B, sum_b.at[p], p)
        sent(COEF_B, put_b.at[0], p)
        sent(SUM_C, sum_c.at[p], p)
        sent(COEF_C, put_c.at[0], p)
        sent(MOBILITY, mob_all.at[group], p)
        store(p).wait()

    over_peers(finish)
    store(group).wait()
    for copy in adj_ring + adj_rim + phase_rim + pot_ring + bar_ring + bar_rim + tuple(mob_copies):
        copy.wait_send()


def body(slabs, phase_noise, labels, solute, mobility, cotangent, adj_solute):
    _, orders, layers, rows, lanes = phase_noise.shape
    sub = labels.shape[0]
    tile = (rows, lanes)

    def vmem(*lead):
        return pltpu.VMEM(lead + tile, jnp.float32)

    anywhere = pl.BlockSpec(memory_space=pl.ANY)
    in_vmem = pl.BlockSpec(memory_space=pltpu.VMEM)
    elements = orders * layers * rows * lanes
    grad, solute_gradient, mobility_gradient = pl.pallas_call(
        functools.partial(kernel, slabs),
        out_shape=(
            jax.ShapeDtypeStruct(phase_noise.shape[1:], jnp.float32),
            jax.ShapeDtypeStruct(solute.shape, jnp.float32),
            jax.ShapeDtypeStruct((1, mobility.shape[0]), jnp.float32),
        ),
        in_specs=[anywhere, anywhere, anywhere, pl.BlockSpec(memory_space=pltpu.SMEM), anywhere, anywhere],
        out_specs=(anywhere, in_vmem, in_vmem),
        scratch_shapes=[
            vmem(orders, layers + 2), vmem(orders, layers + 2), vmem(orders, layers + 2),
            vmem(orders, layers), vmem(orders, layers), vmem(orders, layers), vmem(orders),
            pltpu.VMEM((GROUPS, sub) + tile, jnp.int32),
            vmem(sub), vmem(sub + 2), vmem(sub + 2), vmem(sub + 2),
            vmem(GROUPS, sub), vmem(GROUPS, sub), vmem(2, sub), vmem(GROUPS, sub),
            vmem(GROUPS, 2, sub), vmem(GROUPS, 2, sub), vmem(2, 2, sub), vmem(GROUPS, 2, sub),
            vmem(GROUPS, sub), vmem(GROUPS, sub), vmem(2, sub), vmem(GROUPS, sub),
            pltpu.VMEM((orders, lanes), jnp.float32),
            pltpu.VMEM((max(slabs - 1, 1), orders, lanes), jnp.float32),
            pltpu.VMEM((GROUPS, orders, lanes), jnp.float32),
            pltpu.SemaphoreType.DMA((5,)),
            pltpu.SemaphoreType.DMA((GROUPS,)),
            pltpu.SemaphoreType.DMA((8, GROUPS)),
            pltpu.SemaphoreType.DMA((8, GROUPS)),
            pltpu.SemaphoreType.DMA((6, 2)),
            pltpu.SemaphoreType.DMA((6, 2)),
            pltpu.SemaphoreType.DMA((max(slabs - 1, 1),)),
            pltpu.SemaphoreType.DMA((max(slabs - 1, 1),)),
        ],
        compiler_params=pltpu.CompilerParams(
            collective_id=0, has_side_effects=True, vmem_limit_bytes=24 * 1024 * 1024
        ),
        cost_estimate=pl.CostEstimate(flops=100 * elements, bytes_accessed=12 * elements, transcendentals=0),
    )(phase_noise[0], labels, solute, mobility, cotangent[0], adj_solute)
    return grad[None], solute_gradient, mobility_gradient.reshape(-1)


def solution(mesh):
    slabs = mesh.shape["space"] // GROUPS
    fields = P(("runs", "space"), None, None, None, None)
    cells = P(("runs", "space"), None, None)
    return jax.shard_map(
        functools.partial(body, slabs),
        mesh=mesh,
        in_specs=(fields, cells, cells, P(), fields, cells),
        out_specs=(fields, cells, P("runs")),
        check_vma=False,
    )
```

time: 115 us -> 41.3 us (0.36)
  waiting for transfers between devices: 35 us -> 0 us
  Pallas kernels: 0 us -> 33.6 us
  blocking collectives: 30.8 us -> 0 us
  starting transfers between devices: 27.6 us -> 0 us
  other arithmetic: 18.7 us -> 0 us
  local copies, waits for them, and re-layouts: 1.46 us -> 6.72 us
    ppermute x26 -> x0, waiting for transfers between devices: 35 us -> none  [the longest x18 31.1 us: swapped(): return lax.ppermute(block, axis, route)]
    pallas_call x0 -> x1, Pallas kernels: none -> 33.6 us  [body(): pl.pallas_call(functools.partial(kernel, slabs), out_shape=(jax.ShapeDtyp...]
    psum x1 -> x0, blocking collectives: 30.8 us -> none  [body(): mobility_gradient = lax.psum(placed, 'space')]
    ppermute x26 -> x0, starting transfers between devices: 27.6 us -> none  [the longest x18 15.9 us: swapped(): return lax.ppermute(block, axis, route)]
    unnamed x20 -> x15, local copies, waits for them, and re-layouts: 0.88 us -> 6.72 us
    add x18 -> x0, other arithmetic: 5.28 us -> none  [the longest x3 3.18 us: laplace_rows(): return result + jnp.roll(middle, 1, 3) + jnp.roll(middle, -1, 3)]
    concatenate x15 -> x0, other arithmetic: 5.01 us -> none  [the longest x10 4.37 us: backward_step(): stacked = jnp.concatenate([weighted, adj_conc[None]], 0)]
    reduce_sum x4 -> x0, other arithmetic: 2.92 us -> none  [the longest x1 1.08 us: react(): return reaction + chem_slope * 2.0 * phases * (beta_mask - share) / denom]
  transfers between devices with their start and end apart: 26 -> 0, of which waited for: 15 -> 0; matrix products, arithmetic and copies ran while one was open for 10% -> 0% of each run, Pallas kernels for 0% -> 0%
where the time goes in v1:
time: 41.3 us; the launch traced here: 40.9 us
  Pallas kernels  33.6 us (81%)
  local copies, waits for them, and re-layouts  6.72 us (16%)
  between operations  0.65 us (2%)
    pallas_call x1, Pallas kernels, body(): pl.pallas_call(functools.partial(kernel, slabs), out_shape=(jax.ShapeDtyp...  33.6 us
    unnamed x15, local copies, waits for them, and re-layouts  6.72 us

profile of v1, /device:TPU:0, one launch (start us, length us, event | category | flops | bytes accessed | tf_op | source)
XLA Modules:
  0.0 40.9 jit_solution(18073091612473958753)
XLA Ops:
  0.6 0.0 copy-start.5
  0.6 0.6 %copy-done.5 = f32[64]{0:T(128)S(1)} copy-done((f32[64]{0:T(128)S(1)}, f32[64]{0:T(128)}, u32[]{:S(2)}) %copy-start.5) | copy-done | bytes 280
  1.3 0.0 copy-start
  1.3 1.0 %copy-done = f32[1,8,16,8,128]{4,3,2,1,0:T(8,128)S(1)} copy-done((f32[1,8,16,8,128]{4,3,2,1,0:T(8,128)S(1)}, f32[1,8,16,8,128]{4,3,2,1,0:T(8,128)}, u32[]{:S(2)}) %copy-start) | copy-done | bytes 524312
  2.3 0.0 copy-start.1
  2.3 1.0 %copy-done.1 = f32[1,8,16,8,128]{4,3,2,1,0:T(8,128)S(1)} copy-done((f32[1,8,16,8,128]{4,3,2,1,0:T(8,128)S(1)}, f32[1,8,16,8,128]{4,3,2,1,0:T(8,128)}, u32[]{:S(2)}) %copy-start.1) | copy-done | bytes 524312
  3.4 0.0 copy-start.2
  3.4 0.7 %copy-done.2 = s32[2,8,128]{2,1,0:T(8,128)S(1)} copy-done((s32[2,8,128]{2,1,0:T(8,128)S(1)}, s32[2,8,128]{2,1,0:T(8,128)}, u32[]{:S(2)}) %copy-start.2) | copy-done | bytes 8216
  4.1 0.0 copy-start.3
  4.1 0.7 %copy-done.3 = f32[2,8,128]{2,1,0:T(8,128)S(1)} copy-done((f32[2,8,128]{2,1,0:T(8,128)S(1)}, f32[2,8,128]{2,1,0:T(8,128)}, u32[]{:S(2)}) %copy-start.3) | copy-done | bytes 8216
  4.8 0.0 copy-start.4
  4.8 0.7 %copy-done.4 = f32[2,8,128]{2,1,0:T(8,128)S(1)} copy-done((f32[2,8,128]{2,1,0:T(8,128)S(1)}, f32[2,8,128]{2,1,0:T(8,128)}, u32[]{:S(2)}) %copy-start.4) | copy-done | bytes 8216
  5.5 33.6 %shard_map.85 = (f32[8,16,8,128]{3,2,1,0:T(8,128)S(1)}, f32[2,8,128]{2,1,0:T(8,128)S(1)}, f32[1,64]{1,0:T(1,128)S(1)}) custom-call(f32[8,16,8,128]{3,2,1,0:T(8,128)S(1)} %bitcast.5, s32[2,8,128]{2,1,0:T(8,128)S(1)} %copy-done.2, f32[2,8,128]{2,1,0:T(8,128)S(1)} %copy-done.3, f32[64]{0:T(128)S(1)} %copy-done.5, f32[8,16,8,128]{3,2,1,0:T(8,128)S(1)} %bitcast.6, ...), custom_call_target="tpu_custom_call" | custom-call | flops 13107200 | bytes 1572864 | tf_op jit(solution)/shard_map/pallas_call | solution.py:395
  39.0 0.8 %copy.12 = f32[1,8,16,8,128]{4,3,2,1,0:T(8,128)} copy(f32[1,8,16,8,128]{4,3,2,1,0:T(8,128)S(1)} %bitcast.4) | data formatting | bytes 1048576
  39.8 0.6 %copy.13 = f32[2,8,128]{2,1,0:T(8,128)} copy(f32[2,8,128]{2,1,0:T(8,128)S(1)} %get-tuple-element.13) | data formatting | bytes 16384
  40.4 0.5 %copy.14 = f32[64]{0:T(128)} copy(f32[64]{0:T(128)S(1)} %bitcast.7) | data formatting | bytes 512
Async XLA Ops:
  0.6 0.7 %copy-start.5 = (f32[64]{0:T(128)S(1)}, f32[64]{0:T(128)}, u32[]{:S(2)}) copy-start(f32[64]{0:T(128)} %mobility_ref.1) | copy-start | bytes 772
  1.3 1.0 %copy-start = (f32[1,8,16,8,128]{4,3,2,1,0:T(8,128)S(1)}, f32[1,8,16,8,128]{4,3,2,1,0:T(8,128)}, u32[]{:S(2)}) copy-start(f32[1,8,16,8,128]{4,3,2,1,0:T(8,128)} %param.6) | copy-start | bytes 1572868
  2.3 1.0 %copy-start.1 = (f32[1,8,16,8,128]{4,3,2,1,0:T(8,128)S(1)}, f32[1,8,16,8,128]{4,3,2,1,0:T(8,128)}, u32[]{:S(2)}) copy-start(f32[1,8,16,8,128]{4,3,2,1,0:T(8,128)} %param.10) | copy-start | bytes 1572868
  3.4 0.7 %copy-start.2 = (s32[2,8,128]{2,1,0:T(8,128)S(1)}, s32[2,8,128]{2,1,0:T(8,128)}, u32[]{:S(2)}) copy-start(s32[2,8,128]{2,1,0:T(8,128)} %labels_ref.1) | copy-start | bytes 24580
  4.1 0.7 %copy-start.3 = (f32[2,8,128]{2,1,0:T(8,128)S(1)}, f32[2,8,128]{2,1,0:T(8,128)}, u32[]{:S(2)}) copy-start(f32[2,8,128]{2,1,0:T(8,128)} %solute_ref.1) | copy-start | bytes 24580
  4.8 0.7 %copy-start.4 = (f32[2,8,128]{2,1,0:T(8,128)S(1)}, f32[2,8,128]{2,1,0:T(8,128)}, u32[]{:S(2)}) copy-start(f32[2,8,128]{2,1,0:T(8,128)} %adjc_ref.1) | copy-start | bytes 24580

commit v2 on v1

v2 whole, which is shorter than its diff:
```python
import functools

import jax
import jax.numpy as jnp
from jax import lax
from jax.experimental import pallas as pl
from jax.experimental.pallas import tpu as pltpu
from jax.sharding import PartitionSpec as P

P_SIZE = 64
GROUPS = 8

time_step = 0.1
gradient_coef = 0.75
coupling = 1.5
chem_height = 2.5
alpha_level = 0.2
beta_level = 0.8
solute_mobility = 0.3
epsilon = 1e-05

MESH = pl.DeviceIdType.MESH
CUBIC = 1.0 - 2.0 * coupling
GAP = beta_level - alpha_level
BETA_GROUP = GROUPS // 2
PAIRS = GROUPS // 2
VMEM_LIMIT = 16 * 1024 * 1024

LABELS, SUM_A, COEF_A, SUM_B, COEF_B, SUM_C, COEF_C, MOBILITY = range(8)
PHASE_RIM, ADJ_RIM, BAR_RIM, ADJ_RING, POT_RING, BAR_RING, GIVE, GIVE_BACK = range(8)


def turn(x):
    last = x.ndim - 1
    lanes, rows = x.shape[-1], x.shape[-2]
    across = pltpu.roll(x, 1, last) + pltpu.roll(x, lanes - 1, last)
    return across + (pltpu.roll(x, 1, last - 1) + pltpu.roll(x, rows - 1, last - 1))


def curve(ref, layer):
    middle = ref[:, layer + 1]
    return (ref[:, layer] + ref[:, layer + 2] - 6.0 * middle) + turn(middle)


def curve_cells(ref):
    middle = ref[1:-1]
    return (ref[:-2] + ref[2:] - 6.0 * middle) + turn(middle)


def kernel(
    slabs, noise_ref, labels_ref, solute_ref, mobility_hbm, adj_ref, adjc_ref,
    grad_ref, solgrad_ref, mobgrad_ref,
    mobility_ref, phi, lam, bar, phi1, drive, pre, rate_buf, lab, conc, adjc, pot, adjc1,
    sum_a, got_a, put_a, coef_a, sum_b, got_b, put_b, coef_b, sum_c, got_c, put_c, coef_c,
    mob_mine, mob_slabs, mob_all, solgrad,
    load_sem, send_sem, recv_sem, rim_send, rim_recv, mob_send, mob_recv,
):
    orders, layers = noise_ref.shape[0], noise_ref.shape[1]
    sub = layers // GROUPS
    span = layers // PAIRS
    place = lax.axis_index("space")
    count = slabs * GROUPS
    group = lax.rem(place, GROUPS)
    slab = lax.div(place, GROUPS)
    base = slab * GROUPS
    pair = lax.div(group, 2)
    second = lax.rem(group, 2)
    owner = second == 1
    above, below = lax.rem(place + GROUPS, count), lax.rem(place + count - GROUPS, count)

    def pair_at(j):
        high = lax.rem(lax.div(pair, 2) + lax.div(j, 2), 2)
        low = lax.rem(lax.rem(pair, 2) + lax.rem(j, 2), 2)
        return 2 * high + low

    def far_pairs():
        return [pair_at(jnp.int32(j)) for j in range(PAIRS - 1, 0, -1)]

    def others():
        return [2 * q + c for q in far_pairs() for c in range(2)] + [2 * pair + 1 - second]

    def other_slab(s):
        return lax.rem(slab + s, slabs) * GROUPS + group

    def shifted(by):
        return lax.rem(place + count + by, count)

    barrier = pltpu.get_barrier_semaphore()

    def greet(device):
        pl.semaphore_signal(barrier, inc=1, device_id={"space": device}, device_id_type=MESH)

    for s in range(1, slabs):
        greet(other_slab(s))

    @pl.when(owner)
    def _():
        for by in (2, -2, 1):
            greet(shifted(by))

    for g in others():
        greet(base + g)

    load_labels = pltpu.make_async_copy(labels_ref, lab.at[pl.ds(group * sub, sub)], load_sem.at[0])
    load_noise = pltpu.make_async_copy(noise_ref, phi.at[:, pl.ds(1, layers)], load_sem.at[1])
    load_adjc = pltpu.make_async_copy(adjc_ref, adjc.at[pl.ds(1 + second * sub, sub)], load_sem.at[2])
    load_solute = pltpu.make_async_copy(solute_ref, conc.at[pl.ds(second * sub, sub)], load_sem.at[3])
    load_adj = pltpu.make_async_copy(adj_ref, lam.at[:, pl.ds(1, layers)], load_sem.at[4])
    load_mobility = pltpu.make_async_copy(mobility_hbm, mobility_ref, load_sem.at[5])
    for load in (load_mobility, load_labels, load_noise, load_adjc, load_solute, load_adj):
        load.start()
    load_mobility.wait()
    for i in range(orders):
        rate_buf[i] = jnp.full(rate_buf.shape[1:], time_step * mobility_ref[group * orders + i], jnp.float32)

    pl.semaphore_wait(barrier, GROUPS - 1 + slabs - 1 + 1 + second)

    def to_group(kind, src, dst, g, slot):
        return pltpu.make_async_remote_copy(
            src_ref=src, dst_ref=dst, send_sem=send_sem.at[kind, g], recv_sem=recv_sem.at[kind, slot],
            device_id={"space": base + g}, device_id_type=MESH,
        )

    def arrived(kind, dst, slot):
        to_group(kind, dst, dst, 2 * pair + 1 - second, slot).wait_recv()

    def sent(kind, src, g):
        to_group(kind, src, src, g, g).wait_send()

    def rim_copy(kind, side, src, dst, device):
        return pltpu.make_async_remote_copy(
            src_ref=src, dst_ref=dst, send_sem=rim_send.at[kind, side], recv_sem=rim_recv.at[kind, side],
            device_id={"space": device}, device_id_type=MESH,
        )

    def rims_of(kind, src, ref, offset):
        last = layers + 1
        return (
            rim_copy(kind, 0, src.at[:, layers - 1 + offset], ref.at[:, 0], above),
            rim_copy(kind, 1, src.at[:, offset], ref.at[:, last], below),
        )

    def ring_of(kind, ref):
        return (
            rim_copy(kind, 0, ref.at[span], ref.at[0], shifted(2)),
            rim_copy(kind, 1, ref.at[1], ref.at[span + 1], shifted(-2)),
        )

    sibling = shifted(1 - 2 * second)
    adj_down = rim_copy(ADJ_RING, 1, adjc_ref.at[0], adjc.at[span + 1], shifted(-1))
    adj_up = rim_copy(ADJ_RING, 0, adjc_ref.at[sub - 1], adjc.at[0], shifted(2))
    give_adjc = rim_copy(GIVE, 0, adjc_ref, adjc.at[pl.ds(1, sub)], sibling)
    give_solute = rim_copy(GIVE, 1, solute_ref, conc.at[pl.ds(0, sub)], sibling)
    pot_ring = ring_of(POT_RING, pot)
    bar_ring = ring_of(BAR_RING, adjc1)
    give_solgrad = rim_copy(GIVE_BACK, 0, solgrad.at[pl.ds(0, sub)], solgrad.at[pl.ds(0, sub)], sibling)

    for g in others():
        to_group(LABELS, labels_ref, lab.at[pl.ds(group * sub, sub)], g, group).start()

    @pl.when(owner)
    def _():
        adj_up.start()

    @pl.when(second == 0)
    def _():
        give_solute.start()
        give_adjc.start()
        adj_down.start()

    adj_rim = rims_of(ADJ_RIM, adj_ref, lam, 0)

    def labels_from(g):
        arrived(LABELS, lab.at[pl.ds(g * sub, sub)], g)

    def over_layers(q, act):
        for k in range(span):
            act(q * span + k, k)

    def give_sum(kind, sums, got, q):
        to_group(kind, sums.at[q], got.at[group], 2 * q + 1, group).start()

    def over_pairs(kind, sums, got, chunk, carry):
        def run(i, carry):
            q = pair_at(PAIRS - 1 - i)
            carry = chunk(q, True, carry)
            give_sum(kind, sums, got, q)
            return carry

        carry = lax.fori_loop(0, PAIRS - 1, run, carry)
        carry = chunk(pair, False, carry)

        @pl.when(second == 0)
        def _():
            give_sum(kind, sums, got, pair)

        @pl.when(owner)
        def _():
            got[group] = sums[pair]

        return carry

    def all_sums(kind, got):
        for g in others():
            arrived(kind, got.at[g], g)

    def give_coef(kind, put, coef):
        for g in others():
            to_group(kind, put.at[lax.div(g, BETA_GROUP)], coef.at[pair], g, pair).start()
        coef[pair] = put[lax.div(group, BETA_GROUP)]

    def own_coef(kind, coef):
        @pl.when(second == 0)
        def _():
            arrived(kind, coef.at[pair], pair)

    def start_chunk(q, far, carry):
        if far:
            labels_from(2 * q)
            labels_from(2 * q + 1)
        else:
            labels_from(2 * pair + 1 - second)

        def layer(z, k):
            ids = group * orders + lax.broadcasted_iota(jnp.int32, rate_buf.shape, 0)
            field = phi[:, z + 1] + jnp.where(lab[z][None] == ids, 0.5, 0.0)
            phi[:, z + 1] = field
            sum_a[q, k] = jnp.sum(field * field, axis=0)

        over_layers(q, layer)
        return carry

    load_labels.wait()
    load_noise.wait()
    over_pairs(SUM_A, sum_a, got_a, start_chunk, 0)
    phase_rim = rims_of(PHASE_RIM, phi, phi, 1)
    for copy in phase_rim + adj_rim:
        copy.start()

    def local_drive(z):
        field = phi[:, z + 1]
        drive[:, z] = CUBIC * field * field * field - gradient_coef * curve(phi, z)

    def over_inner(act):
        def run(z, carry):
            act(z)
            return carry

        lax.fori_loop(1, layers - 1, run, 0)

    over_inner(local_drive)
    load_adjc.wait()
    load_solute.wait()
    load_adj.wait()

    def total_of(parts):
        low, high = parts[0], parts[BETA_GROUP]
        for g in range(1, BETA_GROUP):
            low = low + parts[g]
            high = high + parts[BETA_GROUP + g]
        return low + high, high

    def state_of(squares, beta_squares, c):
        inverse = 1.0 / (squares + epsilon)
        share = beta_squares * inverse
        slope = chem_height * ((c - beta_level) ** 2 - (c - alpha_level) ** 2)
        pull = 2.0 * slope * inverse
        plain = 2.0 * coupling * squares - 1.0 - pull * share
        return inverse, share, pull, plain

    def adjoint_of(state, moment, beta_moment, pot_bar):
        inverse, share, pull, _ = state
        scaled = pull * inverse
        pot_part = (2.0 * chem_height * GAP) * inverse * pot_bar
        all_bar = 2.0 * coupling * moment - scaled * (beta_moment - 2.0 * share * moment) + share * pot_part
        beta_bar = -scaled * moment - pot_part
        c_bar = (-4.0 * chem_height * GAP) * inverse * (beta_moment - share * moment) + 2.0 * chem_height * pot_bar
        return 2.0 * all_bar, 2.0 * (all_bar + beta_bar), c_bar

    @pl.when(owner)
    def _():
        give_solute.wait_recv()
        all_sums(SUM_A, got_a)
        state = state_of(*total_of(got_a), conc[...])
        put_a[0] = state[3]
        put_a[1] = state[3] + state[2]
        give_coef(COEF_A, put_a, coef_a)
        pot[1 : span + 1] = 2.0 * chem_height * (conc[...] - alpha_level - state[1] * GAP)
        for copy in pot_ring:
            copy.start()

    for copy in phase_rim:
        copy.wait_recv()
    local_drive(0)
    local_drive(layers - 1)

    def step_chunk(q, far, carry):
        if far:
            arrived(COEF_A, coef_a.at[q], q)
        else:
            own_coef(COEF_A, coef_a)

        def layer(z, k):
            field = phi[:, z + 1]
            full = drive[:, z] + field * coef_a[q, k][None]
            drive[:, z] = full
            rate = rate_buf[...]
            following = field - rate * full
            phi1[:, z] = following
            sum_b[q, 0, k] = jnp.sum(following * following, axis=0)
            sum_b[q, 1, k] = -jnp.sum(rate * lam[:, z + 1] * following, axis=0)

        over_layers(q, layer)
        return carry

    over_pairs(SUM_B, sum_b, got_b, step_chunk, 0)

    def local_bar(z, moved):
        adj, field, rate = lam[:, z + 1], phi1[:, z], rate_buf[...]
        curved = gradient_coef * curve(lam, z)
        squared = field * field
        pre[:, z] = adj + rate * (curved - (3.0 * CUBIC) * squared * adj)
        return moved + field * (CUBIC * squared * adj - curved)

    moved = lax.fori_loop(1, layers - 1, local_bar, jnp.zeros(rate_buf.shape, jnp.float32))

    @pl.when(owner)
    def _():
        for copy in (give_adjc, adj_up, adj_down) + pot_ring:
            copy.wait_recv()
        pot_bar = (time_step * solute_mobility) * curve_cells(adjc)
        conc1 = conc[...] + (time_step * solute_mobility) * curve_cells(pot)
        all_sums(SUM_B, got_b)
        state = state_of(*total_of([got_b[g, 0] for g in range(GROUPS)]), conc1)
        plain, beta, c_bar = adjoint_of(state, *total_of([got_b[g, 1] for g in range(GROUPS)]), pot_bar)
        put_b[0, 0] = state[3]
        put_b[0, 1] = plain
        put_b[1, 0] = state[3] + state[2]
        put_b[1, 1] = beta
        give_coef(COEF_B, put_b, coef_b)
        adjc1[1 : span + 1] = adjc[1 : span + 1] + c_bar
        for copy in bar_ring:
            copy.start()

    for copy in adj_rim:
        copy.wait_recv()
    moved = local_bar(0, moved)
    moved = local_bar(layers - 1, moved)

    def bar_chunk(q, far, moved):
        if far:
            arrived(COEF_B, coef_b.at[q], q)
        else:
            own_coef(COEF_B, coef_b)
        for k in range(span):
            z = q * span + k
            adj, field, rate = lam[:, z + 1], phi1[:, z], rate_buf[...]
            scaled = adj * coef_b[q, 0, k][None]
            full = pre[:, z] + field * coef_b[q, 1, k][None] - rate * scaled
            bar[:, z + 1] = full
            sum_c[q, k] = -jnp.sum(rate * full * phi[:, z + 1], axis=0)
            moved = moved + (field * scaled + full * drive[:, z])
        return moved

    moved = over_pairs(SUM_C, sum_c, got_c, bar_chunk, moved)
    bar_rim = rims_of(BAR_RIM, bar, bar, 1)
    for copy in bar_rim:
        copy.start()
    mob_mine[...] = -time_step * jnp.sum(moved, axis=1)
    mob_copies = [
        pltpu.make_async_remote_copy(
            src_ref=mob_mine, dst_ref=mob_slabs.at[s - 1], send_sem=mob_send.at[s - 1], recv_sem=mob_recv.at[s - 1],
            device_id={"space": other_slab(s)}, device_id_type=MESH,
        )
        for s in range(1, slabs)
    ]
    for copy in mob_copies:
        copy.start()

    def local_grad(z):
        full, field, rate = bar[:, z + 1], phi[:, z + 1], rate_buf[...]
        slope = coef_a[z // span, z % span][None] + (3.0 * CUBIC) * field * field
        pre[:, z] = full + rate * (gradient_coef * curve(bar, z) - full * slope)

    over_inner(local_grad)

    @pl.when(owner)
    def _():
        for copy in bar_ring:
            copy.wait_recv()
        pot_bar = (time_step * solute_mobility) * curve_cells(adjc1)
        state = state_of(*total_of(got_a), conc[...])
        all_sums(SUM_C, got_c)
        plain, beta, c_bar = adjoint_of(state, *total_of(got_c), pot_bar)
        put_c[0] = plain
        put_c[1] = beta
        give_coef(COEF_C, put_c, coef_c)
        solgrad[...] = adjc1[1 : span + 1] + c_bar
        give_solgrad.start()

    for copy in mob_copies:
        copy.wait_recv()
    whole = mob_mine[...]
    for s in range(1, slabs):
        whole = whole + mob_slabs[s - 1]
    mob_all[group] = whole
    for g in others():
        to_group(MOBILITY, mob_all.at[group], mob_all.at[group], g, group).start()

    for copy in bar_rim:
        copy.wait_recv()
    local_grad(0)
    local_grad(layers - 1)

    def grad_chunk(q):
        def layer(z, k):
            grad_ref[:, z] = pre[:, z] + phi[:, z + 1] * coef_c[q, k][None]

        over_layers(q, layer)

    own_coef(COEF_C, coef_c)
    grad_chunk(pair)

    def grad_pair(j, carry):
        q = pair_at(j)
        arrived(COEF_C, coef_c.at[q], q)
        grad_chunk(q)
        return carry

    lax.fori_loop(1, PAIRS, grad_pair, 0)

    @pl.when(second == 0)
    def _():
        give_solgrad.wait_recv()

    solgrad_ref[...] = solgrad[pl.ds(second * sub, sub)]
    for g in others():
        arrived(MOBILITY, mob_all.at[g], g)
    table = mob_all[...].reshape(GROUPS * orders, mob_all.shape[-1])
    mobgrad_ref[...] = jnp.sum(table.T, axis=0, keepdims=True)

    for g in others():
        sent(LABELS, labels_ref, g)
        sent(MOBILITY, mob_all.at[group], g)
    for q in far_pairs():
        sent(SUM_A, sum_a.at[q], 2 * q + 1)
        sent(SUM_B, sum_b.at[q], 2 * q + 1)
        sent(SUM_C, sum_c.at[q], 2 * q + 1)

    @pl.when(second == 0)
    def _():
        for copy in (give_solute, give_adjc, adj_down):
            copy.wait_send()
        sent(SUM_A, sum_a.at[pair], 2 * pair + 1)
        sent(SUM_B, sum_b.at[pair], 2 * pair + 1)
        sent(SUM_C, sum_c.at[pair], 2 * pair + 1)

    @pl.when(owner)
    def _():
        for copy in (adj_up, give_solgrad) + pot_ring + bar_ring:
            copy.wait_send()
        for g in others():
            sent(COEF_A, put_a.at[0], g)
            sent(COEF_B, put_b.at[0], g)
            sent(COEF_C, put_c.at[0], g)

    for copy in adj_rim + phase_rim + bar_rim + tuple(mob_copies):
        copy.wait_send()


def hand_over(grad_in, solute_in, mobility_in, grad_out, solute_out, mobility_out, sem):
    copies = [pltpu.make_async_copy(solute_in, solute_out, sem.at[0])]
    copies.append(pltpu.make_async_copy(mobility_in, mobility_out, sem.at[1]))
    for i in range(grad_in.shape[0]):
        copies.append(pltpu.make_async_copy(grad_in.at[i], grad_out.at[i], sem.at[2 + i]))
    for copy in copies:
        copy.start()
    for copy in copies:
        copy.wait()


def body(slabs, phase_noise, labels, solute, mobility, cotangent, adj_solute):
    _, orders, layers, rows, lanes = phase_noise.shape
    sub = labels.shape[0]
    span = layers // PAIRS
    tile = (rows, lanes)

    def vmem(*lead):
        return pltpu.VMEM(lead + tile, jnp.float32)

    in_hbm = pl.BlockSpec(memory_space=pltpu.HBM)
    in_vmem = pl.BlockSpec(memory_space=pltpu.VMEM)
    elements = orders * layers * rows * lanes
    grad, solute_gradient, mobility_gradient = pl.pallas_call(
        functools.partial(kernel, slabs),
        out_shape=(
            jax.ShapeDtypeStruct(phase_noise.shape[1:], jnp.float32),
            jax.ShapeDtypeStruct(solute.shape, jnp.float32),
            jax.ShapeDtypeStruct((1, mobility.shape[0]), jnp.float32),
        ),
        in_specs=[in_hbm] * 6,
        out_specs=(in_vmem,) * 3,
        scratch_shapes=[
            pltpu.SMEM(mobility.shape, jnp.float32),
            vmem(orders, layers + 2), vmem(orders, layers + 2), vmem(orders, layers + 2),
            vmem(orders, layers), vmem(orders, layers), vmem(orders, layers), vmem(orders),
            pltpu.VMEM((layers,) + tile, jnp.int32),
            vmem(span), vmem(span + 2), vmem(span + 2), vmem(span + 2),
            vmem(PAIRS, span), vmem(GROUPS, span), vmem(2, span), vmem(PAIRS, span),
            vmem(PAIRS, 2, span), vmem(GROUPS, 2, span), vmem(2, 2, span), vmem(PAIRS, 2, span),
            vmem(PAIRS, span), vmem(GROUPS, span), vmem(2, span), vmem(PAIRS, span),
            pltpu.VMEM((orders, lanes), jnp.float32),
            pltpu.VMEM((max(slabs - 1, 1), orders, lanes), jnp.float32),
            pltpu.VMEM((GROUPS, orders, lanes), jnp.float32),
            vmem(span),
            pltpu.SemaphoreType.DMA((6,)),
            pltpu.SemaphoreType.DMA((8, GROUPS)),
            pltpu.SemaphoreType.DMA((8, GROUPS)),
            pltpu.SemaphoreType.DMA((8, 2)),
            pltpu.SemaphoreType.DMA((8, 2)),
            pltpu.SemaphoreType.DMA((max(slabs - 1, 1),)),
            pltpu.SemaphoreType.DMA((max(slabs - 1, 1),)),
        ],
        compiler_params=pltpu.CompilerParams(
            collective_id=0, has_side_effects=True, vmem_limit_bytes=VMEM_LIMIT
        ),
        cost_estimate=pl.CostEstimate(flops=100 * elements, bytes_accessed=12 * elements, transcendentals=0),
    )(*(pltpu.with_memory_space_constraint(x, pltpu.HBM) for x in (phase_noise[0], labels, solute, mobility, cotangent[0], adj_solute)))
    grad, solute_gradient, mobility_gradient = pl.pallas_call(
        hand_over,
        out_shape=tuple(jax.ShapeDtypeStruct(x.shape, x.dtype) for x in (grad, solute_gradient, mobility_gradient)),
        in_specs=[in_vmem] * 3,
        out_specs=(in_hbm,) * 3,
        scratch_shapes=[pltpu.SemaphoreType.DMA((orders + 2,))],
        compiler_params=pltpu.CompilerParams(vmem_limit_bytes=VMEM_LIMIT),
        cost_estimate=pl.CostEstimate(flops=0, bytes_accessed=8 * elements, transcendentals=0),
    )(grad, solute_gradient, mobility_gradient)
    return grad[None], solute_gradient, mobility_gradient.reshape(-1)


def solution(mesh):
    slabs = mesh.shape["space"] // GROUPS
    fields = P(("runs", "space"), None, None, None, None)
    cells = P(("runs", "space"), None, None)
    return jax.shard_map(
        functools.partial(body, slabs),
        mesh=mesh,
        in_specs=(fields, cells, cells, P(), fields, cells),
        out_specs=(fields, cells, P("runs")),
        check_vma=False,
    )
```

time: 41.3 us -> 33.9 us (0.82)
  local copies, waits for them, and re-layouts: 6.72 us -> 0 us
  Pallas kernels: 33.6 us -> 33.1 us
    unnamed x15 -> x0, local copies, waits for them, and re-layouts: 6.72 us -> none
    pallas_call x1, Pallas kernels: 33.6 us -> 32.2 us  [body(): pl.pallas_call(functools.partial(kernel, slabs), out_shape=(jax.ShapeDtyp...]
    pallas_call x0 -> x1, Pallas kernels: none -> 0.88 us  [body(): pl.pallas_call(hand_over, out_shape=tuple((jax.ShapeDtypeStruct(x.shape,...]
where the time goes in v2:
time: 33.9 us; the launch traced here: 33.7 us
  Pallas kernels  33.1 us (98%)
  between operations  0.64 us (2%)
    pallas_call x1, Pallas kernels, body(): pl.pallas_call(functools.partial(kernel, slabs), out_shape=(jax.ShapeDtyp...  32.2 us
    pallas_call x1, Pallas kernels, body(): pl.pallas_call(hand_over, out_shape=tuple((jax.ShapeDtypeStruct(x.shape,...  0.88 us

profile of v2, /device:TPU:0, one launch (start us, length us, event | category | flops | bytes accessed | tf_op | source)
XLA Modules:
  0.0 33.7 jit_solution(5363846679152584774)
XLA Ops:
  0.6 32.2 %shard_map.85 = (f32[8,16,8,128]{3,2,1,0:T(8,128)S(1)}, f32[2,8,128]{2,1,0:T(8,128)S(1)}, f32[1,64]{1,0:T(1,128)S(1)}) custom-call(f32[8,16,8,128]{3,2,1,0:T(8,128)} %bitcast.4, s32[2,8,128]{2,1,0:T(8,128)} %labels_ref.1, f32[2,8,128]{2,1,0:T(8,128)} %solute_ref.1, f32[64]{0:T(128)} %mobility_hbm.1, f32[8,16,8,128]{3,2,1,0:T(8,128)} %bitcast.5, ...), custom_call_target="tpu_custom_call" | custom-call | flops 13107200 | bytes 1572864 | tf_op jit(solution)/shard_map/pallas_call | solution.py:494
  32.9 0.9 %shard_map.86 = (f32[8,16,8,128]{3,2,1,0:T(8,128)}, f32[2,8,128]{2,1,0:T(8,128)}, f32[1,64]{1,0:T(1,128)}) custom-call(f32[8,16,8,128]{3,2,1,0:T(8,128)S(1)} %get-tuple-element.9.grad_in, f32[2,8,128]{2,1,0:T(8,128)S(1)} %get-tuple-element.10.solute_in, f32[1,64]{1,0:T(1,128)S(1)} %get-tuple-element.11.mobility_in), custom_call_target="tpu_custom_call" | custom-call | bytes 1048576 | tf_op jit(solution)/shard_map/pallas_call | solution.py:529

commit v3 on v2

--- a/solution.py
+++ b/solution.py
@@ -26,8 +26,8 @@
 PAIRS = GROUPS // 2
 VMEM_LIMIT = 16 * 1024 * 1024
 
-LABELS, SUM_A, COEF_A, SUM_B, COEF_B, SUM_C, COEF_C, MOBILITY = range(8)
-PHASE_RIM, ADJ_RIM, BAR_RIM, ADJ_RING, POT_RING, BAR_RING, GIVE, GIVE_BACK = range(8)
+LABELS, SUM_A, COEF_A, SUM_B, COEF_B, SUM_C, COEF_C, MOBILITY, SUM_END = range(9)
+PHASE_RIM, ADJ_RIM, BAR_RIM, ADJ_RING, POT_RING, BAR_RING, GIVE, GIVE_BACK, LABEL_RIM = range(9)
 
 
 def turn(x):
@@ -50,7 +50,7 @@
 def kernel(
     slabs, noise_ref, labels_ref, solute_ref, mobility_hbm, adj_ref, adjc_ref,
     grad_ref, solgrad_ref, mobgrad_ref,
-    mobility_ref, phi, lam, bar, phi1, drive, pre, rate_buf, lab, conc, adjc, pot, adjc1,
+    mobility_ref, phi, lam, bar, phi1, drive, pre, rate_buf, lab, lab_rim, conc, adjc, pot, adjc1,
     sum_a, got_a, put_a, coef_a, sum_b, got_b, put_b, coef_b, sum_c, got_c, put_c, coef_c,
     mob_mine, mob_slabs, mob_all, solgrad,
     load_sem, send_sem, recv_sem, rim_send, rim_recv, mob_send, mob_recv,
@@ -168,7 +168,14 @@
         give_adjc.start()
         adj_down.start()
 
+    phase_rim = rims_of(PHASE_RIM, noise_ref, phi, 0)
     adj_rim = rims_of(ADJ_RIM, adj_ref, lam, 0)
+    label_rim = (
+        rim_copy(LABEL_RIM, 0, lab.at[layers - 1], lab_rim.at[0], above),
+        rim_copy(LABEL_RIM, 1, lab.at[0], lab_rim.at[1], below),
+    )
+    for copy in phase_rim:
+        copy.start()
 
     def labels_from(g):
         arrived(LABELS, lab.at[pl.ds(g * sub, sub)], g)
@@ -214,6 +221,12 @@
         def _():
             arrived(kind, coef.at[pair], pair)
 
+    def started(at, label):
+        ids = group * orders + lax.broadcasted_iota(jnp.int32, rate_buf.shape, 0)
+        field = phi[:, at] + jnp.where(label[None] == ids, 0.5, 0.0)
+        phi[:, at] = field
+        return field
+
     def start_chunk(q, far, carry):
         if far:
             labels_from(2 * q)
@@ -222,9 +235,7 @@
             labels_from(2 * pair + 1 - second)
 
         def layer(z, k):
-            ids = group * orders + lax.broadcasted_iota(jnp.int32, rate_buf.shape, 0)
-            field = phi[:, z + 1] + jnp.where(lab[z][None] == ids, 0.5, 0.0)
-            phi[:, z + 1] = field
+            field = started(z + 1, lab[z])
             sum_a[q, k] = jnp.sum(field * field, axis=0)
 
         over_layers(q, layer)
@@ -233,13 +244,43 @@
     load_labels.wait()
     load_noise.wait()
     over_pairs(SUM_A, sum_a, got_a, start_chunk, 0)
-    phase_rim = rims_of(PHASE_RIM, phi, phi, 1)
-    for copy in phase_rim + adj_rim:
+    for copy in label_rim:
         copy.start()
 
-    def local_drive(z):
-        field = phi[:, z + 1]
-        drive[:, z] = CUBIC * field * field * field - gradient_coef * curve(phi, z)
+    def local_layer(z):
+        field, rate = phi[:, z + 1], rate_buf[...]
+        push = CUBIC * field * field * field - gradient_coef * curve(phi, z)
+        drive[:, z] = push
+        known = field - rate * push
+        phi1[:, z] = known
+        scaled, adj = rate * field, rate * lam[:, z + 1]
+        q, k = z // span, z % span
+        sum_b[q, k, 0] = jnp.sum(known * known, axis=0)
+        sum_b[q, k, 1] = jnp.sum(scaled * known, axis=0)
+        sum_b[q, k, 2] = jnp.sum(scaled * scaled, axis=0)
+        sum_b[q, k, 3] = jnp.sum(adj * known, axis=0)
+        sum_b[q, k, 4] = jnp.sum(adj * scaled, axis=0)
+
+    def inner_part(q):
+        first = 1 if q == 0 else 0
+        return pl.ds(first, span - 1 if q in (0, PAIRS - 1) else span)
+
+    def end_part(q):
+        return pl.ds(0 if q == 0 else span - 1, 1)
+
+    def give_part(kind, q, part):
+        @pl.when(2 * q + 1 != group)
+        def _():
+            to_group(kind, sum_b.at[q, part], got_b.at[group, part], 2 * q + 1, group).start()
+
+        @pl.when(2 * q + 1 == group)
+        def _():
+            got_b[group, part] = sum_b[q, part]
+
+    def sent_part(kind, q, part):
+        @pl.when(2 * q + 1 != group)
+        def _():
+            sent(kind, sum_b.at[q, part], 2 * q + 1)
 
     def over_inner(act):
         def run(z, carry):
@@ -248,10 +289,21 @@
 
         lax.fori_loop(1, layers - 1, run, 0)
 
-    over_inner(local_drive)
+    load_adj.wait()
+
+    for q in (0, PAIRS - 1) + tuple(range(1, PAIRS - 1)):
+        first = max(q * span, 1)
+        last = min((q + 1) * span, layers - 1)
+
+        def run(z, carry):
+            local_layer(z)
+            return carry
+
+        lax.fori_loop(first, last, run, 0)
+        give_part(SUM_B, q, inner_part(q))
+
     load_adjc.wait()
     load_solute.wait()
-    load_adj.wait()
 
     def total_of(parts):
         low, high = parts[0], parts[BETA_GROUP]
@@ -289,40 +341,17 @@
         for copy in pot_ring:
             copy.start()
 
-    for copy in phase_rim:
+    for copy in phase_rim + label_rim:
         copy.wait_recv()
-    local_drive(0)
-    local_drive(layers - 1)
-
-    def step_chunk(q, far, carry):
-        if far:
-            arrived(COEF_A, coef_a.at[q], q)
-        else:
-            own_coef(COEF_A, coef_a)
-
-        def layer(z, k):
-            field = phi[:, z + 1]
-            full = drive[:, z] + field * coef_a[q, k][None]
-            drive[:, z] = full
-            rate = rate_buf[...]
-            following = field - rate * full
-            phi1[:, z] = following
-            sum_b[q, 0, k] = jnp.sum(following * following, axis=0)
-            sum_b[q, 1, k] = -jnp.sum(rate * lam[:, z + 1] * following, axis=0)
-
-        over_layers(q, layer)
-        return carry
-
-    over_pairs(SUM_B, sum_b, got_b, step_chunk, 0)
-
-    def local_bar(z, moved):
-        adj, field, rate = lam[:, z + 1], phi1[:, z], rate_buf[...]
-        curved = gradient_coef * curve(lam, z)
-        squared = field * field
-        pre[:, z] = adj + rate * (curved - (3.0 * CUBIC) * squared * adj)
-        return moved + field * (CUBIC * squared * adj - curved)
-
-    moved = lax.fori_loop(1, layers - 1, local_bar, jnp.zeros(rate_buf.shape, jnp.float32))
+    started(0, lab_rim[0])
+    started(layers + 1, lab_rim[1])
+
+    for q in (0, PAIRS - 1):
+        local_layer(q * (layers - 1) // (PAIRS - 1))
+        give_part(SUM_END, q, end_part(q))
+
+    for copy in adj_rim:
+        copy.start()
 
     @pl.when(owner)
     def _():
@@ -330,9 +359,25 @@
             copy.wait_recv()
         pot_bar = (time_step * solute_mobility) * curve_cells(adjc)
         conc1 = conc[...] + (time_step * solute_mobility) * curve_cells(pot)
-        all_sums(SUM_B, got_b)
-        state = state_of(*total_of([got_b[g, 0] for g in range(GROUPS)]), conc1)
-        plain, beta, c_bar = adjoint_of(state, *total_of([got_b[g, 1] for g in range(GROUPS)]), pot_bar)
+        for q in range(PAIRS):
+
+            @pl.when(pair == q)
+            def _():
+                for g in others():
+                    arrived(SUM_B, got_b.at[g, inner_part(q)], g)
+                if q in (0, PAIRS - 1):
+                    for g in others():
+                        arrived(SUM_END, got_b.at[g, end_part(q)], g)
+
+        def plane(first, a):
+            parts = [got_b[first] + got_b[first + 1], got_b[first + 2] + got_b[first + 3]]
+            sums = parts[0] + parts[1]
+            return sums[:, 0] - a * (2.0 * sums[:, 1] - a * sums[:, 2]), a * sums[:, 4] - sums[:, 3]
+
+        low_squares, low_moment = plane(0, put_a[0])
+        squares, moment = plane(BETA_GROUP, put_a[1])
+        state = state_of(low_squares + squares, squares, conc1)
+        plain, beta, c_bar = adjoint_of(state, low_moment + moment, moment, pot_bar)
         put_b[0, 0] = state[3]
         put_b[0, 1] = plain
         put_b[1, 0] = state[3] + state[2]
@@ -342,16 +387,40 @@
         for copy in bar_ring:
             copy.start()
 
+    def step_chunk(q):
+        def layer(z, k):
+            part = phi[:, z + 1] * coef_a[q, k][None]
+            drive[:, z] = drive[:, z] + part
+            phi1[:, z] = phi1[:, z] - rate_buf[...] * part
+
+        over_layers(q, layer)
+
+    own_coef(COEF_A, coef_a)
+    step_chunk(pair)
+
+    def step_pair(j, carry):
+        q = pair_at(j)
+        arrived(COEF_A, coef_a.at[q], q)
+        step_chunk(q)
+        return carry
+
+    lax.fori_loop(1, PAIRS, step_pair, 0)
+
+    def local_bar(z, moved):
+        adj, field, rate = lam[:, z + 1], phi1[:, z], rate_buf[...]
+        curved = gradient_coef * curve(lam, z)
+        squared = field * field
+        pre[:, z] = adj + rate * (curved - (3.0 * CUBIC) * squared * adj)
+        return moved + field * (CUBIC * squared * adj - curved)
+
+    moved = lax.fori_loop(1, layers - 1, local_bar, jnp.zeros(rate_buf.shape, jnp.float32))
+
     for copy in adj_rim:
         copy.wait_recv()
     moved = local_bar(0, moved)
     moved = local_bar(layers - 1, moved)
 
-    def bar_chunk(q, far, moved):
-        if far:
-            arrived(COEF_B, coef_b.at[q], q)
-        else:
-            own_coef(COEF_B, coef_b)
+    def bar_chunk(q, moved):
         for k in range(span):
             z = q * span + k
             adj, field, rate = lam[:, z + 1], phi1[:, z], rate_buf[...]
@@ -362,10 +431,27 @@
             moved = moved + (field * scaled + full * drive[:, z])
         return moved
 
-    moved = over_pairs(SUM_C, sum_c, got_c, bar_chunk, moved)
     bar_rim = rims_of(BAR_RIM, bar, bar, 1)
-    for copy in bar_rim:
-        copy.start()
+
+    def end_pair_sums(q):
+        @pl.when(2 * q + 1 != group)
+        def _():
+            give_sum(SUM_C, sum_c, got_c, q)
+
+        @pl.when(2 * q + 1 == group)
+        def _():
+            got_c[group] = sum_c[q]
+
+    for step, q in enumerate((PAIRS - 1, 0) + tuple(range(1, PAIRS - 1))):
+
+        @pl.when(2 * q + 1 != group)
+        def _():
+            arrived(COEF_B, coef_b.at[q], q)
+
+        moved = bar_chunk(q, moved)
+        end_pair_sums(q)
+        if step < 2:
+            bar_rim[step].start()
     mob_mine[...] = -time_step * jnp.sum(moved, axis=1)
     mob_copies = [
         pltpu.make_async_remote_copy(
@@ -439,12 +525,15 @@
     table = mob_all[...].reshape(GROUPS * orders, mob_all.shape[-1])
     mobgrad_ref[...] = jnp.sum(table.T, axis=0, keepdims=True)
 
+    for q in range(PAIRS):
+        sent_part(SUM_B, q, inner_part(q))
+        if q in (0, PAIRS - 1):
+            sent_part(SUM_END, q, end_part(q))
     for g in others():
         sent(LABELS, labels_ref, g)
         sent(MOBILITY, mob_all.at[group], g)
     for q in far_pairs():
         sent(SUM_A, sum_a.at[q], 2 * q + 1)
-        sent(SUM_B, sum_b.at[q], 2 * q + 1)
         sent(SUM_C, sum_c.at[q], 2 * q + 1)
 
     @pl.when(second == 0)
@@ -452,7 +541,6 @@
         for copy in (give_solute, give_adjc, adj_down):
             copy.wait_send()
         sent(SUM_A, sum_a.at[pair], 2 * pair + 1)
-        sent(SUM_B, sum_b.at[pair], 2 * pair + 1)
         sent(SUM_C, sum_c.at[pair], 2 * pair + 1)
 
     @pl.when(owner)
@@ -464,7 +552,7 @@
             sent(COEF_B, put_b.at[0], g)
             sent(COEF_C, put_c.at[0], g)
 
-    for copy in adj_rim + phase_rim + bar_rim + tuple(mob_copies):
+    for copy in adj_rim + phase_rim + label_rim + bar_rim + tuple(mob_copies):
         copy.wait_send()
 
 
@@ -504,20 +592,20 @@
             pltpu.SMEM(mobility.shape, jnp.float32),
             vmem(orders, layers + 2), vmem(orders, layers + 2), vmem(orders, layers + 2),
             vmem(orders, layers), vmem(orders, layers), vmem(orders, layers), vmem(orders),
-            pltpu.VMEM((layers,) + tile, jnp.int32),
+            pltpu.VMEM((layers,) + tile, jnp.int32), pltpu.VMEM((2,) + tile, jnp.int32),
             vmem(span), vmem(span + 2), vmem(span + 2), vmem(span + 2),
             vmem(PAIRS, span), vmem(GROUPS, span), vmem(2, span), vmem(PAIRS, span),
-            vmem(PAIRS, 2, span), vmem(GROUPS, 2, span), vmem(2, 2, span), vmem(PAIRS, 2, span),
+            vmem(PAIRS, span, 5), vmem(GROUPS, span, 5), vmem(2, 2, span), vmem(PAIRS, 2, span),
             vmem(PAIRS, span), vmem(GROUPS, span), vmem(2, span), vmem(PAIRS, span),
             pltpu.VMEM((orders, lanes), jnp.float32),
             pltpu.VMEM((max(slabs - 1, 1), orders, lanes), jnp.float32),
             pltpu.VMEM((GROUPS, orders, lanes), jnp.float32),
             vmem(span),
             pltpu.SemaphoreType.DMA((6,)),
-            pltpu.SemaphoreType.DMA((8, GROUPS)),
-            pltpu.SemaphoreType.DMA((8, GROUPS)),
-            pltpu.SemaphoreType.DMA((8, 2)),
-            pltpu.SemaphoreType.DMA((8, 2)),
+            pltpu.SemaphoreType.DMA((9, GROUPS)),
+            pltpu.SemaphoreType.DMA((9, GROUPS)),
+            pltpu.SemaphoreType.DMA((9, 2)),
+            pltpu.SemaphoreType.DMA((9, 2)),
             pltpu.SemaphoreType.DMA((max(slabs - 1, 1),)),
             pltpu.SemaphoreType.DMA((max(slabs - 1, 1),)),
         ],

time: 33.9 us -> 31.3 us (0.923)
  Pallas kernels: 33.1 us -> 30.5 us
    pallas_call x1, Pallas kernels: 32.2 us -> 29.6 us  [body(): pl.pallas_call(functools.partial(kernel, slabs), out_shape=(jax.ShapeDtyp...]
where the time goes in v3:
time: 31.3 us; the launch traced here: 31.2 us
  Pallas kernels  30.5 us (97%)
  between operations  0.64 us (2%)
    pallas_call x1, Pallas kernels, body(): pl.pallas_call(functools.partial(kernel, slabs), out_shape=(jax.ShapeDtyp...  29.6 us
    pallas_call x1, Pallas kernels, body(): pl.pallas_call(hand_over, out_shape=tuple((jax.ShapeDtypeStruct(x.shape,...  0.88 us

profile of v3, /device:TPU:0, one launch (start us, length us, event | category | flops | bytes accessed | tf_op | source)
XLA Modules:
  0.0 31.2 jit_solution(16427465202088067138)
XLA Ops:
  0.6 29.6 %shard_map.85 = (f32[8,16,8,128]{3,2,1,0:T(8,128)S(1)}, f32[2,8,128]{2,1,0:T(8,128)S(1)}, f32[1,64]{1,0:T(1,128)S(1)}) custom-call(f32[8,16,8,128]{3,2,1,0:T(8,128)} %bitcast.4, s32[2,8,128]{2,1,0:T(8,128)} %labels_ref.1, f32[2,8,128]{2,1,0:T(8,128)} %solute_ref.1, f32[64]{0:T(128)} %mobility_hbm.1, f32[8,16,8,128]{3,2,1,0:T(8,128)} %bitcast.5, ...), custom_call_target="tpu_custom_call" | custom-call | flops 13107200 | bytes 1572864 | tf_op jit(solution)/shard_map/pallas_call | solution.py:582
  30.3 0.9 %shard_map.86 = (f32[8,16,8,128]{3,2,1,0:T(8,128)}, f32[2,8,128]{2,1,0:T(8,128)}, f32[1,64]{1,0:T(1,128)}) custom-call(f32[8,16,8,128]{3,2,1,0:T(8,128)S(1)} %get-tuple-element.9.grad_in, f32[2,8,128]{2,1,0:T(8,128)S(1)} %get-tuple-element.10.solute_in, f32[1,64]{1,0:T(1,128)S(1)} %get-tuple-element.11.mobility_in), custom_call_target="tpu_custom_call" | custom-call | bytes 1048576 | tf_op jit(solution)/shard_map/pallas_call | solution.py:617

commit v4 on v3

--- a/solution.py
+++ b/solution.py
@@ -336,7 +336,6 @@
         state = state_of(*total_of(got_a), conc[...])
         put_a[0] = state[3]
         put_a[1] = state[3] + state[2]
-        give_coef(COEF_A, put_a, coef_a)
         pot[1 : span + 1] = 2.0 * chem_height * (conc[...] - alpha_level - state[1] * GAP)
         for copy in pot_ring:
             copy.start()
@@ -352,6 +351,10 @@
 
     for copy in adj_rim:
         copy.start()
+
+    @pl.when(owner)
+    def _():
+        give_coef(COEF_A, put_a, coef_a)
 
     @pl.when(owner)
     def _():

time: 31.3 us -> 30.4 us (0.971)
  Pallas kernels: 30.5 us -> 29.6 us
    pallas_call x1, Pallas kernels: 29.6 us -> 28.7 us  [body(): pl.pallas_call(functools.partial(kernel, slabs), out_shape=(jax.ShapeDtyp...]
where the time goes in v4:
time: 30.4 us; the launch traced here: 30.2 us
  Pallas kernels  29.6 us (97%)
  between operations  0.64 us (2%)
    pallas_call x1, Pallas kernels, body(): pl.pallas_call(functools.partial(kernel, slabs), out_shape=(jax.ShapeDtyp...  28.7 us
    pallas_call x1, Pallas kernels, body(): pl.pallas_call(hand_over, out_shape=tuple((jax.ShapeDtypeStruct(x.shape,...  0.88 us

profile of v4, /device:TPU:0, one launch (start us, length us, event | category | flops | bytes accessed | tf_op | source)
XLA Modules:
  0.0 30.2 jit_solution(12481998346929986752)
XLA Ops:
  0.6 28.7 %shard_map.85 = (f32[8,16,8,128]{3,2,1,0:T(8,128)S(1)}, f32[2,8,128]{2,1,0:T(8,128)S(1)}, f32[1,64]{1,0:T(1,128)S(1)}) custom-call(f32[8,16,8,128]{3,2,1,0:T(8,128)} %bitcast.4, s32[2,8,128]{2,1,0:T(8,128)} %labels_ref.1, f32[2,8,128]{2,1,0:T(8,128)} %solute_ref.1, f32[64]{0:T(128)} %mobility_hbm.1, f32[8,16,8,128]{3,2,1,0:T(8,128)} %bitcast.5, ...), custom_call_target="tpu_custom_call" | custom-call | flops 13107200 | bytes 1572864 | tf_op jit(solution)/shard_map/pallas_call | solution.py:585
  29.3 0.9 %shard_map.86 = (f32[8,16,8,128]{3,2,1,0:T(8,128)}, f32[2,8,128]{2,1,0:T(8,128)}, f32[1,64]{1,0:T(1,128)}) custom-call(f32[8,16,8,128]{3,2,1,0:T(8,128)S(1)} %get-tuple-element.9.grad_in, f32[2,8,128]{2,1,0:T(8,128)S(1)} %get-tuple-element.10.solute_in, f32[1,64]{1,0:T(1,128)S(1)} %get-tuple-element.11.mobility_in), custom_call_target="tpu_custom_call" | custom-call | bytes 1048576 | tf_op jit(solution)/shard_map/pallas_call | solution.py:620

commit v5 on v4

--- a/solution.py
+++ b/solution.py
@@ -234,6 +234,14 @@
         else:
             labels_from(2 * pair + 1 - second)
 
+        @pl.when(q == PAIRS - 1)
+        def _():
+            label_rim[0].start()
+
+        @pl.when(q == 0)
+        def _():
+            label_rim[1].start()
+
         def layer(z, k):
             field = started(z + 1, lab[z])
             sum_a[q, k] = jnp.sum(field * field, axis=0)
@@ -244,8 +252,6 @@
     load_labels.wait()
     load_noise.wait()
     over_pairs(SUM_A, sum_a, got_a, start_chunk, 0)
-    for copy in label_rim:
-        copy.start()
 
     def local_layer(z):
         field, rate = phi[:, z + 1], rate_buf[...]

time: 30.4 us -> 30.5 us (level)
  no operation moved by 1% of the time
where the time goes in v5:
time: 30.5 us; the launch traced here: 30.4 us
  Pallas kernels  29.8 us (98%)
  between operations  0.64 us (2%)
    pallas_call x1, Pallas kernels, body(): pl.pallas_call(functools.partial(kernel, slabs), out_shape=(jax.ShapeDtyp...  28.9 us
    pallas_call x1, Pallas kernels, body(): pl.pallas_call(hand_over, out_shape=tuple((jax.ShapeDtypeStruct(x.shape,...  0.88 us

profile of v5, /device:TPU:0, one launch (start us, length us, event | category | flops | bytes accessed | tf_op | source)
XLA Modules:
  0.0 30.4 jit_solution(5649752177332511039)
XLA Ops:
  0.6 28.9 %shard_map.85 = (f32[8,16,8,128]{3,2,1,0:T(8,128)S(1)}, f32[2,8,128]{2,1,0:T(8,128)S(1)}, f32[1,64]{1,0:T(1,128)S(1)}) custom-call(f32[8,16,8,128]{3,2,1,0:T(8,128)} %bitcast.4, s32[2,8,128]{2,1,0:T(8,128)} %labels_ref.1, f32[2,8,128]{2,1,0:T(8,128)} %solute_ref.1, f32[64]{0:T(128)} %mobility_hbm.1, f32[8,16,8,128]{3,2,1,0:T(8,128)} %bitcast.5, ...), custom_call_target="tpu_custom_call" | custom-call | flops 13107200 | bytes 1572864 | tf_op jit(solution)/shard_map/pallas_call | solution.py:591
  29.5 0.9 %shard_map.86 = (f32[8,16,8,128]{3,2,1,0:T(8,128)}, f32[2,8,128]{2,1,0:T(8,128)}, f32[1,64]{1,0:T(1,128)}) custom-call(f32[8,16,8,128]{3,2,1,0:T(8,128)S(1)} %get-tuple-element.9.grad_in, f32[2,8,128]{2,1,0:T(8,128)S(1)} %get-tuple-element.10.solute_in, f32[1,64]{1,0:T(1,128)S(1)} %get-tuple-element.11.mobility_in), custom_call_target="tpu_custom_call" | custom-call | bytes 1048576 | tf_op jit(solution)/shard_map/pallas_call | solution.py:626
